TPU v7x, 128 devices: a whole 4x4x4 slice. The times are simulated.
128 devices in a mesh: dp: 16 (over z, y), ctx: 2 (over x_hi), tp: 4 (over x_lo, core).
Axes of the slice: x: 4 (x_hi: 2, x_lo: 2; x = x_hi * 2 + x_lo), y: 4, z: 4, core: 2. Of those that a mesh axis runs over, the one named last changes fastest.
Arguments:
- stream: bfloat16 [16, 2048, 768], P('dp', 'ctx'), may hold values from -6 to 6
- norm_gain: bfloat16 [768], P('dp'), may hold values from 0.5 to 1.5
- w_gate: bfloat16 [768, 1536], P('dp', 'tp'), may hold values from -0.21875 to 0.21875
- w_value: bfloat16 [768, 1536], P('dp', 'tp'), may hold values from -0.21875 to 0.21875
- w_step: bfloat16 [768, 24], P('dp', 'tp'), may hold values from -0.21875 to 0.21875
- w_state: bfloat16 [768, 256], P('dp'), may hold values from -0.21875 to 0.21875
- w_out: bfloat16 [1536, 768], P('tp', 'dp'), may hold values from -0.15625 to 0.15625
- conv_value: float32 [4, 1536], P(None, 'tp'), may hold values from -3 to 3
- conv_value_bias: float32 [1536], P('tp'), may hold values from -3 to 3
- conv_state: float32 [4, 256], replicated, may hold values from -3 to 3
- conv_state_bias: float32 [256], replicated, may hold values from -3 to 3
- step_bias: float32 [24], P('tp'), may hold values from -5 to -1
- decay_log: float32 [24], P('tp'), may hold values from -5 to 0.5
- skip_gain: float32 [24], P('tp'), may hold values from 0.5 to 1.5
- inner_gain: float32 [1536], P('tp'), may hold values from 0.5 to 1.5
- cotangent: bfloat16 [16, 2048, 768], P('dp', 'ctx'), may hold values from -6 to 6
Outputs:
- mixed_out: bfloat16 [16, 2048, 768], P('dp', 'ctx')
- d_stream: float32 [16, 2048, 768], P('dp', 'ctx')
- grad_norm_gain: float32 [768], P('dp')
- grad_w_gate: float32 [768, 1536], P('dp', 'tp')
- grad_w_value: float32 [768, 1536], P('dp', 'tp')
- grad_w_step: float32 [768, 24], P('dp', 'tp')
- grad_w_state: float32 [768, 256], P('dp')
- grad_w_out: float32 [1536, 768], P('tp', 'dp')
- grad_conv_value: float32 [4, 1536], P(None, 'tp')
- grad_conv_value_bias: float32 [1536], P('tp')
- grad_conv_state: float32 [4, 256], replicated
- grad_conv_state_bias: float32 [256], replicated
- grad_step_bias: float32 [24], P('tp')
- grad_decay_log: float32 [24], P('tp')
- grad_skip_gain: float32 [24], P('tp')
- grad_inner_gain: float32 [1536], P('tp')
All inputs are finite; a program needn't handle non-finite values.
Results may differ from a plain program's by a relative error of at most 0.0095.
The roundings to bfloat16 on the way count: a program that leaves them out, or rounds other values in their place, can miss the bound.
Values may be sent and summed in bfloat16 or wider, within the bound.
A program may use at most 128 MiB of HBM per device.

v0:
```python
import jax
import jax.numpy as jnp
from jax import lax
from jax.experimental import pallas as pl
from jax.experimental.pallas import tpu as pltpu
from jax.sharding import PartitionSpec as P

D = 768
HEAD = 64
STATE = 128
CONV = 4
GROUP = 256
INNER = 1536


EPS = 1e-05
HIGH = lax.Precision.HIGHEST


MESH = pl.DeviceIdType.MESH
VM = pl.BlockSpec(memory_space=pltpu.VMEM)
SIDE = 4
ROWS = 48
WIDE = 1536
DMA = pltpu.SemaphoreType.DMA
F32 = jnp.float32
BF16 = jnp.bfloat16


def params(ident, limit=40):
    return pltpu.CompilerParams(
        collective_id=ident, has_side_effects=True, vmem_limit_bytes=limit * 1024 * 1024
    )


def remote(source, target, send, recv, where):
    return pltpu.make_async_remote_copy(
        src_ref=source,
        dst_ref=target,
        send_sem=send,
        recv_sem=recv,
        device_id=where,
        device_id_type=MESH,
    )


def greet(peers):
    barrier = pltpu.get_barrier_semaphore()
    for where in peers:
        pl.semaphore_signal(barrier, inc=1, device_id=where, device_id_type=MESH)
    pl.semaphore_wait(barrier, len(peers))


def place():
    me = lax.axis_index("dp")
    z, y = lax.div(me, SIDE), lax.rem(me, SIDE)

    def along_y(hop):
        return {"dp": z * SIDE + lax.rem(y + hop, SIDE)}

    def along_z(hop):
        return {"dp": lax.rem(z + hop, SIDE) * SIDE + y}

    return z, y, along_y, along_z


def ahead(position, hop):
    return lax.rem(position + hop, SIDE)


class RingGather:
    def __init__(self, block, source, position, along, send, recv, first):
        self.block, self.position, self.along = block, position, along
        self.send, self.recv, self.first = send, recv, first
        self.direct = [
            self.copy(source(0), position, 0, 0, 1),
            self.copy(source(1), position, 1, 1, 3),
            self.copy(source(1), position, 1, 2, 1),
            self.copy(source(0), position, 0, 3, 3),
        ]
        for item in self.direct:
            item.start()

    def copy(self, source, position, sub, slot, hop):
        slot = self.first + slot
        return remote(
            source,
            self.block(position, sub),
            self.send.at[slot],
            self.recv.at[slot],
            self.along(hop),
        )

    def relay(self):
        left, right = ahead(self.position, 3), ahead(self.position, 1)
        self.direct[0].wait_recv()
        one = self.copy(self.block(left, 0), left, 0, 4, 1)
        one.start()
        self.direct[1].wait_recv()
        two = self.copy(self.block(right, 1), right, 1, 5, 3)
        two.start()
        self.relayed = [one, two]

    def finish(self):
        for item in self.direct[2:] + self.relayed:
            item.wait_recv()
        for item in self.direct + self.relayed:
            item.wait_send()


def gather_kernel(shard, edge, full, edge_in, send, recv, own):
    z, y, along_y, along_z = place()
    partner = {"ctx": 1 - lax.axis_index("ctx")}
    greet([along_y(1), along_y(3), along_z(1), along_z(3), partner])
    quarter = WIDE // 4

    def columns(sub):
        return pl.ds(sub * quarter, quarter)

    halo = remote(edge, edge_in, send.at[24], recv.at[24], partner)
    first_y = RingGather(
        lambda at, sub: full.at[z, at, :, columns(sub)],
        lambda sub: shard.at[:, columns(sub)],
        y, along_y, send, recv, 0,
    )
    first_z = RingGather(
        lambda at, sub: full.at[at, y, :, columns(2 + sub)],
        lambda sub: shard.at[:, columns(2 + sub)],
        z, along_z, send, recv, 6,
    )
    halo.start()
    keep = pltpu.make_async_copy(shard, full.at[z, y], own)
    keep.start()
    keep.wait()
    first_y.relay()
    first_z.relay()
    first_y.finish()
    second_z = RingGather(
        lambda at, sub: full.at[at, :, :, columns(sub)],
        lambda sub: full.at[z, :, :, columns(sub)],
        z, along_z, send, recv, 12,
    )
    first_z.finish()
    second_y = RingGather(
        lambda at, sub: full.at[:, at, :, columns(2 + sub)],
        lambda sub: full.at[:, y, :, columns(2 + sub)],
        y, along_y, send, recv, 18,
    )
    second_z.relay()
    second_y.relay()
    second_z.finish()
    second_y.finish()
    halo.wait()


def gather_weights(shard, edge):
    full, edge_in = pl.pallas_call(
        gather_kernel,
        out_shape=(
            jax.ShapeDtypeStruct((SIDE, SIDE, ROWS, WIDE), shard.dtype),
            jax.ShapeDtypeStruct(edge.shape, edge.dtype),
        ),
        in_specs=[VM, VM],
        out_specs=(VM, VM),
        scratch_shapes=[DMA((25,)), DMA((25,)), DMA],
        compiler_params=params(1),
    )(shard, edge)
    return full.reshape(SIDE * SIDE * ROWS, WIDE), edge_in


class RingScatter:
    def __init__(self, block, load, held, passed, position, along, send, recv, first):
        self.block, self.load, self.held, self.passed = block, load, held, passed
        self.position, self.along = position, along
        self.send, self.recv, self.first = send, recv, first
        far, right, left = ahead(position, 2), ahead(position, 1), ahead(position, 3)
        self.direct = [
            self.copy(block(far, 0), 0, 1),
            self.copy(block(far, 1), 1, 3),
            self.copy(block(right, 1), 2, 1),
            self.copy(block(left, 0), 3, 3),
        ]
        for item in self.direct:
            item.start()

    def copy(self, source, slot, hop):
        return remote(
            source,
            self.held.at[slot],
            self.send.at[self.first + slot],
            self.recv.at[self.first + slot],
            self.along(hop),
        )

    def relay(self):
        right, left = ahead(self.position, 1), ahead(self.position, 3)
        self.direct[0].wait_recv()
        self.passed[0] = (self.held[0].astype(F32) + self.load(right, 0).astype(F32)).astype(BF16)
        one = self.copy(self.passed.at[0], 4, 1)
        one.start()
        self.direct[1].wait_recv()
        self.passed[1] = (self.held[1].astype(F32) + self.load(left, 1).astype(F32)).astype(BF16)
        two = self.copy(self.passed.at[1], 5, 3)
        two.start()
        self.relayed = [one, two]

    def total(self, sub):
        own = self.load(self.position, sub).astype(F32)
        if sub == 0:
            self.direct[3].wait_recv()
            self.relayed[0].wait_recv()
            return own + self.held[3].astype(F32) + self.held[4].astype(F32)
        self.direct[2].wait_recv()
        self.relayed[1].wait_recv()
        return own + self.held[2].astype(F32) + self.held[5].astype(F32)

    def finish(self):
        for item in self.direct + self.relayed:
            item.wait_send()


class PairSum:
    def __init__(self, part, out, half_in, over_out, over_in, send, recv, first):
        self.part, self.out = part, out
        self.half_in, self.over_out, self.over_in = half_in, over_out, over_in
        self.send, self.recv, self.first = send, recv, first
        me = lax.axis_index("tp")
        core, chip = lax.rem(me, 2), lax.div(me, 2)
        self.twin, self.across = {"tp": me + 1 - 2 * core}, {"tp": me + 2 - 4 * chip}
        size = part.shape[0] // 4

        def quarter(c, h):
            return pl.ds(pl.multiple_of((2 * c + h) * size, size), size)

        self.keep, self.give = quarter(core, chip), quarter(core, 1 - chip)
        self.sends = [
            self.copy(part.at[quarter(1 - core, 1 - chip)], half_in.at[0], 0, self.twin),
            self.copy(part.at[quarter(1 - core, chip)], half_in.at[1], 1, self.twin),
        ]

    def copy(self, source, target, slot, where):
        item = remote(
            source, target, self.send.at[self.first + slot], self.recv.at[self.first + slot], where
        )
        item.start()
        return item

    def cross(self):
        self.sends[0].wait_recv()
        self.over_out[...] = (
            self.part[self.give].astype(F32) + self.half_in[0].astype(F32)
        ).astype(BF16)
        self.sends.append(self.copy(self.over_out, self.over_in, 2, self.across))

    def close(self, base=None):
        self.sends[1].wait_recv()
        self.sends[2].wait_recv()
        total = self.part[self.keep].astype(F32) + self.half_in[1].astype(F32)
        total = total + self.over_in[...].astype(F32)
        if base is not None:
            total = total + base[self.keep].astype(F32)
        self.out[self.keep] = total.astype(BF16)
        mine = self.out.at[self.keep]
        self.sends.append(self.copy(mine, mine, 3, self.across))
        self.sends.append(self.copy(mine, mine, 4, self.twin))

    def relay(self):
        self.sends[3].wait_recv()
        other = self.out.at[self.give]
        self.sends.append(self.copy(other, other, 5, self.twin))

    def finish(self):
        self.sends[4].wait_recv()
        self.sends[5].wait_recv()
        for item in self.sends:
            item.wait_send()


def pair_scratch(rows, columns):
    return [
        pltpu.VMEM((2, rows // 4, columns), BF16),
        pltpu.VMEM((rows // 4, columns), BF16),
        pltpu.VMEM((rows // 4, columns), BF16),
    ]


def all_peers(along_y, along_z):
    me, partner = lax.axis_index("tp"), {"ctx": 1 - lax.axis_index("ctx")}
    hops = range(1, SIDE)
    tp_peers = [{"tp": ahead(me, hop)} for hop in hops]
    return [along_y(hop) for hop in hops], [along_z(hop) for hop in hops], partner, tp_peers


def spread(source, held, own, peers, send, recv, first):
    copies = [
        remote(source, held.at[own], send.at[first + hop], recv.at[first + hop], peer)
        for hop, peer in enumerate(peers)
    ]
    for item in copies:
        item.start()
    return copies


def fold(held, own, value, copies):
    held[own] = value
    for item in copies:
        item.wait_recv()
    return (held[0] + held[1]) + (held[2] + held[3])


def final_kernel(
    grads, last_grads, small, part, branch, base, out, small_out, normed_out, mixed_out,
    held_z, held_y, held_2z, held_2y, pass_z, pass_y, pass_2z, pass_2y, mid_z, mid_y,
    own_bf, pair_in, small_y, small_z, small_c, small_t, small_now,
    half_0, over_out_0, over_in_0, half_1, over_out_1, over_in_1,
    send, recv, small_send, small_recv, tp_send, tp_recv
):
    z, y, along_y, along_z = place()
    tp = lax.axis_index("tp")
    y_peers, z_peers, partner, tp_peers = all_peers(along_y, along_z)
    greet(y_peers + z_peers + [partner] + tp_peers)
    quarter, half = WIDE // 4, WIDE // 2

    def columns(sub):
        return pl.ds(sub * quarter, quarter)

    normed = PairSum(part, normed_out, half_0, over_out_0, over_in_0, tp_send, tp_recv, 0)
    first_z = RingScatter(
        lambda at, sub: grads.at[at, :, :, columns(sub)],
        lambda at, sub: grads[at, :, :, columns(sub)],
        held_z, pass_z, z, along_z, send, recv, 0,
    )
    first_y = RingScatter(
        lambda at, sub: last_grads.at[:, at] if sub else grads.at[:, at, :, columns(2)],
        lambda at, sub: last_grads[:, at] if sub else grads[:, at, :, columns(2)],
        held_y, pass_y, y, along_y, send, recv, 6,
    )
    mixed = PairSum(branch, mixed_out, half_1, over_out_1, over_in_1, tp_send, tp_recv, 6)
    to_y = spread(small, small_y, y, y_peers, small_send, small_recv, 0)
    normed.cross()
    first_z.relay()
    first_y.relay()
    small_now[0] = fold(small_y, y, small[...], to_y)
    to_z = spread(small_now.at[0], small_z, z, z_peers, small_send, small_recv, 3)
    mixed.cross()
    normed.close()
    for sub in range(2):
        mid_z[:, :, sub * quarter : (sub + 1) * quarter] = first_z.total(sub).astype(BF16)
    second_y = RingScatter(
        lambda at, sub: mid_z.at[at, :, columns(sub)],
        lambda at, sub: mid_z[at, :, columns(sub)],
        held_2y, pass_2y, y, along_y, send, recv, 12,
    )
    for sub in range(2):
        mid_y[:, :, sub * quarter : (sub + 1) * quarter] = first_y.total(sub).astype(BF16)
    second_z = RingScatter(
        lambda at, sub: mid_y.at[at, :, columns(sub)],
        lambda at, sub: mid_y[at, :, columns(sub)],
        held_2z, pass_2z, z, along_z, send, recv, 18,
    )
    small_now[1] = fold(small_z, z, small_now[0], to_z)
    to_ctx = remote(small_now.at[1], small_c, small_send.at[6], small_recv.at[6], partner)
    to_ctx.start()
    second_y.relay()
    second_z.relay()
    mixed.close(base)
    for sub in range(2):
        own_bf[:, sub * quarter : (sub + 1) * quarter] = second_y.total(sub).astype(BF16)
    for sub in range(2):
        own_bf[:, half + sub * quarter : half + (sub + 1) * quarter] = second_z.total(sub).astype(
            BF16
        )
    pair = remote(own_bf, pair_in, send.at[24], recv.at[24], partner)
    pair.start()
    to_ctx.wait_recv()
    small_now[2] = small_now[1] + small_c[...]
    shared = pl.ds(16, 8)
    to_tp = spread(small_now.at[2, shared], small_t, tp, tp_peers, small_send, small_recv, 7)
    normed.relay()
    pair.wait_recv()
    out[...] = own_bf[...].astype(F32) + pair_in[...].astype(F32)
    small_out[0:16] = small_now[2, 0:16]
    small_out[16:24] = fold(small_t, tp, small_now[2, 16:24], to_tp)
    mixed.relay()
    normed.finish()
    mixed.finish()
    for item in (first_z, first_y, second_y, second_z):
        item.finish()
    for item in to_y + to_z + to_tp + [to_ctx, pair]:
        item.wait_send()


def final_sums(grads, last_grads, small, part, branch, base):
    rows, columns = part.shape
    quarter = WIDE // 4
    return pl.pallas_call(
        final_kernel,
        out_shape=(
            jax.ShapeDtypeStruct((ROWS, WIDE), F32),
            jax.ShapeDtypeStruct(small.shape, F32),
            jax.ShapeDtypeStruct(part.shape, BF16),
            jax.ShapeDtypeStruct(part.shape, BF16),
        ),
        in_specs=[VM] * 6,
        out_specs=(VM,) * 4,
        scratch_shapes=[
            pltpu.VMEM((6, SIDE, ROWS, quarter), BF16),
            pltpu.VMEM((6, SIDE, ROWS, quarter), BF16),
            pltpu.VMEM((6, ROWS, quarter), BF16),
            pltpu.VMEM((6, ROWS, quarter), BF16),
            pltpu.VMEM((2, SIDE, ROWS, quarter), BF16),
            pltpu.VMEM((2, SIDE, ROWS, quarter), BF16),
            pltpu.VMEM((2, ROWS, quarter), BF16),
            pltpu.VMEM((2, ROWS, quarter), BF16),
            pltpu.VMEM((SIDE, ROWS, 2 * quarter), BF16),
            pltpu.VMEM((SIDE, ROWS, 2 * quarter), BF16),
            pltpu.VMEM((ROWS, WIDE), BF16),
            pltpu.VMEM((ROWS, WIDE), BF16),
            pltpu.VMEM((SIDE, *small.shape), F32),
            pltpu.VMEM((SIDE, *small.shape), F32),
            pltpu.VMEM(small.shape, F32),
            pltpu.VMEM((SIDE, 8, small.shape[1]), F32),
            pltpu.VMEM((3, *small.shape), F32),
            *pair_scratch(rows, columns),
            *pair_scratch(rows, columns),
            DMA((25,)),
            DMA((25,)),
            DMA((10,)),
            DMA((10,)),
            DMA((12,)),
            DMA((12,)),
        ],
        compiler_params=params(2),
    )(
        grads.reshape(SIDE, SIDE, ROWS, 3 * quarter),
        last_grads.reshape(SIDE, SIDE, ROWS, quarter),
        small,
        part,
        branch,
        base,
    )


def sum_all_kernel(part, out, held, send, recv):
    me = lax.axis_index("tp")
    peers = [{"tp": ahead(me, hop)} for hop in range(1, SIDE)]
    greet(peers)
    copies = spread(part, held, me, peers, send, recv, 0)
    out[...] = fold(held, me, part[...], copies)
    for item in copies:
        item.wait_send()


def sum_all(part, ident):
    return pl.pallas_call(
        sum_all_kernel,
        out_shape=jax.ShapeDtypeStruct(part.shape, part.dtype),
        in_specs=[VM],
        out_specs=VM,
        scratch_shapes=[pltpu.VMEM((4, *part.shape), part.dtype), DMA((3,)), DMA((3,))],
        compiler_params=params(ident),
    )(part)


def state_sum_kernel(part, values, slopes, out, values_in, slopes_in, state_in, half, over_out, over_in,
                     send, recv):
    partner = {"ctx": 1 - lax.axis_index("ctx")}
    me = lax.axis_index("tp")
    core, chip = lax.rem(me, 2), lax.div(me, 2)
    greet([{"tp": me + 1 - 2 * core}, {"tp": me + 2 - 4 * chip}, partner])
    total = PairSum(part, out, half, over_out, over_in, send, recv, 0)
    early = [
        remote(values, values_in, send.at[6], recv.at[6], partner),
        remote(slopes, slopes_in, send.at[7], recv.at[7], partner),
    ]
    for item in early:
        item.start()
    total.cross()
    total.close()
    total.relay()
    total.finish()
    late = remote(out.at[0:16], state_in, send.at[8], recv.at[8], partner)
    late.start()
    for item in early + [late]:
        item.wait()


def state_sum(part, values, slopes):
    rows, columns = part.shape
    return pl.pallas_call(
        state_sum_kernel,
        out_shape=(
            jax.ShapeDtypeStruct(part.shape, BF16),
            jax.ShapeDtypeStruct(values.shape, values.dtype),
            jax.ShapeDtypeStruct(slopes.shape, slopes.dtype),
            jax.ShapeDtypeStruct((16, columns), BF16),
        ),
        in_specs=[VM] * 3,
        out_specs=(VM,) * 4,
        scratch_shapes=[*pair_scratch(rows, columns), DMA((9,)), DMA((9,))],
        compiler_params=params(7),
    )(part, values, slopes)


LOCAL = 384
MIX = LOCAL + 2 * STATE
THIN = MIX + LOCAL
PROJ = THIN + 128
PAIRS = 3


def dot(left, right, left_dim=1, right_dim=0, precision=None):
    return lax.dot_general(
        left,
        right,
        (((left_dim,), (right_dim,)), ((), ())),
        preferred_element_type=F32,
        precision=precision,
    )


def lanes(rows, columns=128):
    return lax.broadcasted_iota(jnp.int32, (rows, columns), 1)


def expand(per_head):
    first = lanes(per_head.shape[0]) < HEAD
    return jnp.concatenate(
        [
            jnp.where(first, per_head[:, 2 * j : 2 * j + 1], per_head[:, 2 * j + 1 : 2 * j + 2])
            for j in range(PAIRS)
        ],
        axis=1,
    )


def head_sums(wide):
    lane = lanes(wide.shape[0])
    total = jnp.zeros(lane.shape, F32)
    for j in range(PAIRS):
        pair = wide[:, 128 * j : 128 * j + 128]
        even = jnp.sum(jnp.where(lane < HEAD, pair, 0.0), axis=1, keepdims=True)
        odd = jnp.sum(jnp.where(lane < HEAD, 0.0, pair), axis=1, keepdims=True)
        total = jnp.where(lane == 2 * j, even, jnp.where(lane == 2 * j + 1, odd, total))
    return total


def by_head(row, states):
    return jnp.concatenate(
        [row[:, h : h + 1] * states[HEAD * h : HEAD * h + HEAD] for h in range(2 * PAIRS)], axis=0
    )


def lower():
    shape = (GROUP, GROUP)
    return lax.broadcasted_iota(jnp.int32, shape, 0) >= lax.broadcasted_iota(jnp.int32, shape, 1)


def decay_of(cum, cum_t, h, mask):
    return jnp.exp(jnp.where(mask, cum[:, h : h + 1] - cum_t[h : h + 1], -1e30))


def project_kernel(ctx, stream, edge, full, conv, heads, normed_o, pre_o, slope_o, vals_o, gate_o,
                   step_o, sig_o, cum_o, cum_t_o, step_t_o, fresh_o, state_o, gain_o, padded):
    step = pl.program_id(0)

    def normalise(rows):
        scale = lax.rsqrt(jnp.mean(rows * rows, axis=-1, keepdims=True) + EPS)
        return (rows * scale * gain_o[0:1]).astype(BF16)

    @pl.when(step == 0)
    def _():
        gain_o[...] = jnp.broadcast_to(full[:, THIN:PROJ].astype(F32).T[6:7], gain_o.shape)
        rows = dot(normalise(edge[...].astype(F32)), full[:, :MIX])
        rows = rows * jnp.where(ctx[0] == 1, 1.0, 0.0)
        padded[0:8] = rows[8:16].astype(BF16).astype(F32)
        state_o[...] = jnp.zeros_like(state_o)

    @pl.when(step > 0)
    def _():
        padded[0:8] = padded[GROUP : GROUP + 8]

    normed = normalise(stream[...].astype(F32))
    normed_o[...] = normed
    projected = dot(normed, full[:, :PROJ])
    gate_o[...] = projected[:, MIX:THIN]
    pre = projected[:, :MIX].astype(BF16)
    pre_o[...] = pre
    padded[8:] = pre.astype(F32)
    conv_sum = conv[4:5] + sum(conv[k : k + 1] * padded[5 + k : 5 + k + GROUP] for k in range(CONV))
    sig = jax.nn.sigmoid(conv_sum)
    slope_o[...] = sig * (1.0 + conv_sum * (1.0 - sig))
    vals = (conv_sum * sig).astype(BF16)
    vals_o[...] = vals
    live = lanes(GROUP) < 2 * PAIRS
    raw = jnp.where(live, projected[:, THIN:PROJ] + heads[0:1], 0.0)
    sig_o[...] = jnp.where(live, jax.nn.sigmoid(raw), 0.0)
    step_val = jnp.maximum(raw, 0.0) + jnp.log1p(jnp.exp(-jnp.abs(raw)))
    step_val = jnp.where(live, step_val, 0.0)
    step_o[...] = step_val
    log_rate = -jnp.exp(heads[1:2]) * step_val
    cum = dot(lower().astype(F32), log_rate, precision=HIGH)
    cum_o[...] = cum
    cum_t_o[0] = cum.T[0:8]
    step_t_o[0] = step_val.T[0:8]
    last = cum[GROUP - 1 :]
    scales = step_val * jnp.exp(last - cum)
    weighted = (vals[:, :LOCAL].astype(F32) * expand(scales)).astype(BF16)
    fresh = dot(weighted, vals[:, LOCAL : LOCAL + STATE], 0, 0)
    fresh_o[0] = fresh
    state_o[...] = by_head(jnp.exp(last), state_o[...]) + fresh


def inside_kernel(vals, cum, cum_t, step_t, heads, up, full, local_o, back_o):
    back_o[...] = dot(up[...], full[:, PROJ:])
    keys, reads = vals[:, LOCAL : LOCAL + STATE], vals[:, LOCAL + STATE :]
    inner = dot(reads, keys, 1, 1)
    mask, first = lower(), lanes(GROUP) < HEAD
    skip = expand(heads[2:3])
    for j in range(PAIRS):
        here = slice(128 * j, 128 * j + 128)
        pair = vals[:, here]
        outs = []
        for h in (2 * j, 2 * j + 1):
            weights = inner * decay_of(cum, cum_t[0], h, mask) * step_t[0, h : h + 1]
            outs.append(dot(weights.astype(BF16), pair))
        local_o[:, here] = jnp.where(first, outs[0], outs[1]) + skip[:, here] * pair.astype(F32)


def sum_row(wide):
    folded = wide[:, :128] + wide[:, 128:256] + wide[:, 256:]
    return jnp.sum(folded.T, axis=0, keepdims=True)


def output_kernel(vals, local, gate, fresh, cum, entering, back, gain, ssd_o, states_o, sums_o,
                  state):
    @pl.when(pl.program_id(0) == 0)
    def _():
        state[...] = entering[...]

    here = state[...]
    states_o[0] = here
    state[...] = by_head(jnp.exp(cum[GROUP - 1 :]), here) + fresh[0]
    carried = dot(vals[:, LOCAL + STATE :], here.astype(BF16), 1, 1)
    ssd = local[...] + expand(jnp.exp(cum[...])) * carried
    ssd_o[...] = ssd
    gated = ssd * (gate[...] * jax.nn.sigmoid(gate[...]))
    sums_o[0:1] = sum_row(gated * gated)
    sums_o[1:2] = sum_row(back[...] * gain[...] * gated)
    sums_o[2:8] = jnp.zeros((6, GROUP), F32)


def gates_kernel(ssd, gate, back, sums, gain, vals, cum, normal_o, dy_o, dgate_o, read_o, chain_o,
                 dgain_o):
    @pl.when(pl.program_id(0) == 0)
    def _():
        chain_o[...] = jnp.zeros_like(chain_o)
        dgain_o[...] = jnp.zeros_like(dgain_o)

    both = sums[...].T
    scale = lax.rsqrt(both[:, 0:1] / INNER + EPS)
    gate_val, ssd_val = gate[...], ssd[...]
    sig = jax.nn.sigmoid(gate_val)
    act = gate_val * sig
    gated = ssd_val * act
    normal_o[...] = (gated * scale * gain[...]).astype(BF16)
    grad_normal = back[...]
    dgain_o[0:1] += jnp.sum(grad_normal * gated * scale, axis=0, keepdims=True)
    dgated = scale * (grad_normal * gain[...]) - gated * (scale * scale * scale) * (
        both[:, 1:2] / INNER
    )
    dy = (dgated * act).astype(BF16)
    dy_o[...] = dy
    dgate_o[...] = (dgated * ssd_val * (sig * (1.0 + gate_val * (1.0 - sig)))).astype(BF16)
    carried = (dy.astype(F32) * expand(jnp.exp(cum[...]))).astype(BF16)
    read = dot(carried, vals[:, LOCAL + STATE :], 0, 0)
    read_o[0] = read
    chain_o[...] = by_head(jnp.exp(cum[GROUP - 1 :]), chain_o[...]) + read


def split_dot(wide, low, left_dim):
    high = wide.astype(BF16)
    rest = (wide - high.astype(F32)).astype(BF16)
    return dot(high, low, left_dim) + dot(rest, low, left_dim)


def blocks_kernel(dy, vals, cum, cum_t, step_val, step_t, normal, up, full, states, heads, dval_o,
                  dcum_o, dstep_o, dstate_o, branch_o, dout_o, skip_o, total, skips, rows):
    step = pl.program_id(0)

    @pl.when(step == 0)
    def _():
        total[...] = jnp.zeros_like(total)
        skips[...] = jnp.zeros_like(skips)
        rows[...] = jnp.zeros_like(rows)

    branch_o[...] = dot(normal[...], full[:, PROJ:], 1, 1).astype(BF16)
    total[...] += dot(up[...], normal[...], 0, 0)
    dy_f, values_f = dy[...].astype(F32), vals[:, :LOCAL].astype(F32)
    skips[0:1] += jnp.sum(dy_f * values_f, axis=0, keepdims=True)
    keys, reads = vals[:, LOCAL : LOCAL + STATE], vals[:, LOCAL + STATE :]
    inner = dot(reads, keys, 1, 1)
    mask, lane = lower(), lanes(GROUP)
    first = lane < HEAD
    skip = expand(heads[2:3])
    dinner = jnp.zeros((GROUP, GROUP), F32)
    dcum = jnp.zeros((GROUP, 128), F32)
    for j in range(PAIRS):
        here = slice(128 * j, 128 * j + 128)
        pair, dy_pair = values_f[:, here], dy[:, here]
        outs = []
        for h in (2 * j, 2 * j + 1):
            own = jnp.where(first if h % 2 == 0 else ~first, pair, 0.0).astype(BF16)
            decays = decay_of(cum, cum_t[0], h, mask)
            scaled = dot(dy_pair, own, 1, 1) * decays
            step_row = step_t[0, h : h + 1]
            product = scaled * inner
            rows[h : h + 1] = jnp.sum(product, axis=0, keepdims=True)
            dcum = jnp.where(
                lane == h, jnp.sum(product * step_row, axis=1, keepdims=True), dcum
            )
            dinner = dinner + scaled * step_row
            outs.append(dot((inner * decays * step_row).astype(BF16), dy_pair, 0, 0))
        dval_o[:, here] = jnp.where(first, outs[0], outs[1]) + skip[:, here] * dy_f[:, here]
    dstep = rows[...].T
    dstep_o[...] = dstep
    low = states[0].astype(BF16)
    grad_exp = dy_f * expand(jnp.exp(cum[...]))
    dcum_o[...] = dcum - dstep * step_val[...] + head_sums(grad_exp * dot(reads, low, 1, 1))
    dstate_o[:, :STATE] = split_dot(dinner, reads, 0)
    dstate_o[:, STATE:] = dot(grad_exp.astype(BF16), low) + split_dot(dinner, keys, 1)

    @pl.when(step == pl.num_programs(0) - 1)
    def _():
        dout_o[...] = total[...].astype(BF16)
        skip_o[...] = head_sums(skips[...])


def states_kernel(vals, cum, step_val, sig, states, read, arriving, heads, dval, dcum, dstep, dstate,
                  dval_o, state_o, low_o, heads_o, carry):
    @pl.when(pl.program_id(0) == 0)
    def _():
        carry[...] = arriving[...]
        heads_o[...] = jnp.zeros_like(heads_o)

    out = carry[...]
    last = cum[GROUP - 1 :]
    decay = jnp.exp(last)
    carry[...] = by_head(decay, out) + read[0]
    product = out * states[0]
    row = lanes(1)
    dlast = jnp.zeros((1, 128), F32)
    for h in range(2 * PAIRS):
        own = jnp.sum(product[HEAD * h : HEAD * h + HEAD], axis=0, keepdims=True)
        dlast = jnp.where(row == h, jnp.sum(own, axis=1, keepdims=True), dlast)
    dlast = dlast * decay
    fresh = out.astype(BF16)
    keys = vals[:, LOCAL : LOCAL + STATE]
    values_f = vals[:, :LOCAL].astype(F32)
    to_end = jnp.exp(last - cum[...])
    scales = step_val[...] * to_end
    wide = expand(scales)
    dweighted = dot(keys, fresh, 1, 1)
    dval_o[...] = dval[...] + dweighted * wide
    state_o[:, :STATE] = (
        dstate[:, :STATE] + dot((values_f * wide).astype(BF16), fresh)
    ).astype(BF16)
    state_o[:, STATE:] = dstate[:, STATE:].astype(BF16)
    dscales = head_sums(dweighted * values_f)
    spill = dscales * scales
    dlast = dlast + jnp.sum(spill, axis=0, keepdims=True)
    at_end = lax.broadcasted_iota(jnp.int32, (GROUP, 128), 0) == GROUP - 1
    full_cum = dcum[...] - spill + jnp.where(at_end, dlast, 0.0)
    drate = dot(lower().astype(F32), full_cum, 0, 0, precision=HIGH)
    rate = jnp.exp(heads[1:2])
    total_step = dstep[...] + dscales * to_end - rate * drate
    pre = total_step * sig[...]
    low_o[...] = pre.astype(BF16)
    heads_o[0:1] += jnp.sum(pre, axis=0, keepdims=True)
    heads_o[1:2] += -rate * jnp.sum(drate * step_val[...], axis=0, keepdims=True)


def weights_kernel(where, dval, state, slope, pre, dgate, dstep, normed, stream, full, gain, conv,
                   values_next, state_next, slope_next, dgain, heads, skip,
                   part_o, dw_o, small_o, padded, total):
    step = pl.program_id(0)
    block = pl.num_programs(0) - 1 - step

    @pl.when(step == 0)
    def _():
        small_o[...] = jnp.zeros_like(small_o)
        ahead_of = jnp.concatenate([values_next[0:8], state_next[...].astype(F32)[0:8]], axis=1)
        padded[GROUP:] = ahead_of * slope_next[0:8] * jnp.where(where[0] == 0, 1.0, 0.0)
        padded[GROUP:] = jnp.where(
            lax.broadcasted_iota(jnp.int32, (8, MIX), 0) < CONV - 1, padded[GROUP:], 0.0
        )
        total[...] = jnp.zeros_like(total)

    @pl.when(step > 0)
    def _():
        padded[GROUP:] = padded[0:8]

    grad = jnp.concatenate([dval[...], state[...].astype(F32)], axis=1) * slope[...]
    padded[0:GROUP] = grad
    pre_f = pre[...].astype(F32)
    dinput = jnp.zeros((GROUP, MIX), F32)
    for k in range(CONV):
        moved = padded[CONV - 1 - k : CONV - 1 - k + GROUP]
        dinput = dinput + conv[k : k + 1] * moved
        taps = jnp.sum(moved * pre_f, axis=0, keepdims=True)
        small_o[k : k + 1] += taps[:, :LOCAL]
        small_o[6 + k : 7 + k, : 2 * STATE] += taps[:, LOCAL:]
    bias = jnp.sum(grad, axis=0, keepdims=True)
    small_o[4:5] += bias[:, :LOCAL]
    small_o[10:11, : 2 * STATE] += bias[:, LOCAL:]
    low = dinput.astype(BF16)
    rest = [dgate[...], dstep[...]]
    total[...] += dot(normed[...], jnp.concatenate([low] + rest, axis=1), 0, 0)
    share = jnp.where(where[1] == block, 1.0, 0.0)
    once = (dinput[:, LOCAL:] * share).astype(BF16)
    part = dot(jnp.concatenate([low[:, :LOCAL], once] + rest, axis=1), full[:, :PROJ], 1, 1)
    part_o[...] = part.astype(BF16)
    source = stream[...].astype(F32)
    scale = lax.rsqrt(jnp.mean(source * source, axis=-1, keepdims=True) + EPS)
    dnorm = jnp.sum(part * source * scale, axis=0, keepdims=True)
    small_o[16:17] += dnorm[:, :LOCAL]
    small_o[17:18] += dnorm[:, LOCAL:]

    @pl.when(block == 0)
    def _():
        small_o[5:6] = dgain[0:1]
        small_o[11:12, :128] = heads[0:1]
        small_o[12:13, :128] = heads[1:2]
        small_o[13:14, :128] = skip[0:1]
        dw_o[...] = total[...].astype(BF16)


def stream_kernel(normed, stream, up, gain, out):
    source, grad = stream[...].astype(F32), normed[...].astype(F32)
    scale = lax.rsqrt(jnp.mean(source * source, axis=-1, keepdims=True) + EPS)
    scaled = grad * gain[0:1]
    inner = jnp.sum(scaled * source, axis=1, keepdims=True) / D
    out[...] = up[...].astype(F32) + (
        scale * scaled - source * (scale * scale * scale) * inner
    )


BLOCKS = 4


def tokens_spec(columns, backward=False):
    return pl.BlockSpec((GROUP, columns), (lambda g: (BLOCKS - 1 - g, 0)) if backward else (lambda g: (g, 0)))


def cube_spec(rows, columns, backward=False):
    return pl.BlockSpec(
        (1, rows, columns), (lambda g: (BLOCKS - 1 - g, 0, 0)) if backward else (lambda g: (g, 0, 0))
    )


def row_spec(rows, backward=False):
    return pl.BlockSpec((rows, GROUP), (lambda g: (0, BLOCKS - 1 - g)) if backward else (lambda g: (0, g)))


def whole(*shape):
    return pl.BlockSpec(shape, lambda g: (0,) * len(shape))


SCALARS = pl.BlockSpec(memory_space=pltpu.SMEM)


def on_blocks(kernel, ins, outs, scratch, operands):
    return pl.pallas_call(
        kernel,
        grid=(BLOCKS,),
        in_specs=ins,
        out_specs=tuple(spec for spec, shape, dtype in outs),
        out_shape=tuple(jax.ShapeDtypeStruct(shape, dtype) for spec, shape, dtype in outs),
        scratch_shapes=scratch,
        compiler_params=pltpu.CompilerParams(vmem_limit_bytes=48 * 1024 * 1024),
    )(*operands)


def per_device(
    stream,
    norm_gain,
    w_gate,
    w_value,
    w_step,
    w_state,
    w_out,
    conv_value,
    conv_value_bias,
    conv_state,
    conv_state_bias,
    step_bias,
    decay_log,
    skip_gain,
    inner_gain,
    cotangent,
):
    count = stream.shape[1]
    heads_here = step_bias.shape[0]
    ctx, tp = lax.axis_index("ctx"), lax.axis_index("tp")
    rows, up = stream[0], cotangent[0]
    shard = jnp.concatenate(
        [
            w_value,
            w_state,
            w_gate,
            w_step,
            norm_gain[:, None],
            jnp.zeros((ROWS, 128 - heads_here - 1), BF16),
            w_out.T,
        ],
        axis=1,
    )
    conv = jnp.concatenate(
        [
            jnp.concatenate([conv_value, conv_value_bias[None]], axis=0),
            jnp.concatenate([conv_state, conv_state_bias[None]], axis=0),
        ],
        axis=1,
    )
    conv = jnp.pad(conv, ((0, 3), (0, 0)))
    heads = jnp.pad(
        jnp.stack([step_bias, decay_log, skip_gain]), ((0, 5), (0, 128 - heads_here))
    )
    gain_one = inner_gain[None]
    where = jnp.stack([ctx, tp]).astype(jnp.int32)
    full, edge = gather_weights(shard, rows[count - 16 :])

    def tokens_out(columns, dtype=F32, backward=False):
        return (tokens_spec(columns, backward), (count, columns), dtype)

    def cube_out(size, columns, backward=False):
        return (cube_spec(size, columns, backward), (BLOCKS, size, columns), F32)

    def whole_out(size, columns, dtype=F32):
        return (whole(size, columns), (size, columns), dtype)

    full_spec, heads_spec = whole(D, WIDE), whole(8, 128)
    (
        normed, pre, slope, vals, gate, step_val, sig, cum, cum_t, step_t, fresh, leaving, gain_zero
    ) = on_blocks(
        project_kernel,
        [SCALARS, tokens_spec(D), whole(16, D), full_spec, whole(8, MIX), heads_spec],
        [
            tokens_out(D, BF16),
            tokens_out(MIX, BF16),
            tokens_out(MIX),
            tokens_out(MIX, BF16),
            tokens_out(LOCAL),
            tokens_out(128),
            tokens_out(128),
            tokens_out(128),
            cube_out(8, GROUP),
            cube_out(8, GROUP),
            cube_out(LOCAL, STATE),
            whole_out(LOCAL, STATE),
            whole_out(8, D),
        ],
        [pltpu.VMEM((GROUP + 8, MIX), F32)],
        (where, rows, edge, full, conv, heads),
    )
    entering = lax.ppermute(leaving, "ctx", [(0, 1)])
    local, back = on_blocks(
        inside_kernel,
        [
            tokens_spec(MIX),
            tokens_spec(128),
            cube_spec(8, GROUP),
            cube_spec(8, GROUP),
            heads_spec,
            tokens_spec(D),
            full_spec,
        ],
        [tokens_out(LOCAL), tokens_out(LOCAL)],
        [],
        (vals, cum, cum_t, step_t, heads, up, full),
    )
    ssd, states, sums = on_blocks(
        output_kernel,
        [
            tokens_spec(MIX),
            tokens_spec(LOCAL),
            tokens_spec(LOCAL),
            cube_spec(LOCAL, STATE),
            tokens_spec(128),
            whole(LOCAL, STATE),
            tokens_spec(LOCAL),
            whole(1, LOCAL),
        ],
        [tokens_out(LOCAL), cube_out(LOCAL, STATE), (row_spec(8), (8, count), F32)],
        [pltpu.VMEM((LOCAL, STATE), F32)],
        (vals, local, gate, fresh, cum, entering, back, gain_one),
    )
    sums = sum_all(sums, 4)
    normal, dy, dgate, read, returning, dgain = on_blocks(
        gates_kernel,
        [
            tokens_spec(LOCAL, True),
            tokens_spec(LOCAL, True),
            tokens_spec(LOCAL, True),
            row_spec(8, True),
            whole(1, LOCAL),
            tokens_spec(MIX, True),
            tokens_spec(128, True),
        ],
        [
            tokens_out(LOCAL, BF16, True),
            tokens_out(LOCAL, BF16, True),
            tokens_out(LOCAL, BF16, True),
            cube_out(LOCAL, STATE, True),
            whole_out(LOCAL, STATE),
            whole_out(8, LOCAL),
        ],
        [],
        (ssd, gate, back, sums, gain_one, vals, cum),
    )
    arriving = lax.ppermute(returning, "ctx", [(1, 0)])
    dval, dcum, dstep, dstate, branch, dout, skip = on_blocks(
        blocks_kernel,
        [
            tokens_spec(LOCAL),
            tokens_spec(MIX),
            tokens_spec(128),
            cube_spec(8, GROUP),
            tokens_spec(128),
            cube_spec(8, GROUP),
            tokens_spec(LOCAL),
            tokens_spec(D),
            full_spec,
            cube_spec(LOCAL, STATE),
            heads_spec,
        ],
        [
            tokens_out(LOCAL),
            tokens_out(128),
            tokens_out(128),
            tokens_out(2 * STATE),
            tokens_out(D, BF16),
            whole_out(D, LOCAL, BF16),
            whole_out(8, 128),
        ],
        [
            pltpu.VMEM((D, LOCAL), F32),
            pltpu.VMEM((8, LOCAL), F32),
            pltpu.VMEM((128, GROUP), F32),
        ],
        (dy, vals, cum, cum_t, step_val, step_t, normal, up, full, states, heads),
    )
    dval, state_part, dstep_low, head_rows = on_blocks(
        states_kernel,
        [
            tokens_spec(MIX, True),
            tokens_spec(128, True),
            tokens_spec(128, True),
            tokens_spec(128, True),
            cube_spec(LOCAL, STATE, True),
            cube_spec(LOCAL, STATE, True),
            whole(LOCAL, STATE),
            heads_spec,
            tokens_spec(LOCAL, True),
            tokens_spec(128, True),
            tokens_spec(128, True),
            tokens_spec(2 * STATE, True),
        ],
        [
            tokens_out(LOCAL, F32, True),
            tokens_out(2 * STATE, BF16, True),
            tokens_out(128, BF16, True),
            whole_out(8, 128),
        ],
        [pltpu.VMEM((LOCAL, STATE), F32)],
        (vals, cum, step_val, sig, states, read, arriving, heads, dval, dcum, dstep, dstate),
    )
    state_total, values_next, slope_next, state_next = state_sum(
        state_part, dval[:16], slope[:16]
    )
    part, dw, small = on_blocks(
        weights_kernel,
        [
            SCALARS,
            tokens_spec(LOCAL, True),
            tokens_spec(2 * STATE, True),
            tokens_spec(MIX, True),
            tokens_spec(MIX, True),
            tokens_spec(LOCAL, True),
            tokens_spec(128, True),
            tokens_spec(D, True),
            tokens_spec(D, True),
            full_spec,
            whole(8, D),
            whole(8, MIX),
            whole(16, LOCAL),
            whole(16, 2 * STATE),
            whole(16, MIX),
            whole(8, LOCAL),
            heads_spec,
            heads_spec,
        ],
        [tokens_out(D, BF16, True), whole_out(D, PROJ, BF16), whole_out(24, LOCAL)],
        [pltpu.VMEM((GROUP + 8, MIX), F32), pltpu.VMEM((D, PROJ), F32)],
        (
            where, dval, state_total, slope, pre, dgate, dstep_low, normed, rows, full, gain_zero,
            conv, values_next, state_next, slope_next, dgain, head_rows, skip,
        ),
    )
    owned, totals, dnormed, mixed = final_sums(dw, dout, small, part, branch, rows)
    (d_stream,) = on_blocks(
        stream_kernel,
        [tokens_spec(D), tokens_spec(D), tokens_spec(D), whole(8, D)],
        [tokens_out(D)],
        [],
        (dnormed, rows, up, gain_zero),
    )
    gain_total = totals[16:18].reshape(D)
    return (
        mixed[None],
        d_stream[None],
        lax.dynamic_slice_in_dim(gain_total, lax.axis_index("dp") * ROWS, ROWS),
        owned[:, MIX:THIN],
        owned[:, :LOCAL],
        owned[:, THIN : THIN + heads_here],
        owned[:, LOCAL:MIX],
        owned[:, PROJ:].T,
        totals[:4],
        totals[4],
        totals[6:10, : 2 * STATE],
        totals[10, : 2 * STATE],
        totals[11, :heads_here],
        totals[12, :heads_here],
        totals[13, :heads_here],
        totals[5],
    )


def solution(mesh):
    in_specs = (
        P("dp", "ctx", None),
        P("dp"),
        P("dp", "tp"),
        P("dp", "tp"),
        P("dp", "tp"),
        P("dp", None),
        P("tp", "dp"),
        P(None, "tp"),
        P("tp"),
        P(),
        P(),
        P("tp"),
        P("tp"),
        P("tp"),
        P("tp"),
        P("dp", "ctx", None),
    )
    out_specs = (
        P("dp", "ctx", None),
        P("dp", "ctx", None),
        P("dp"),
        P("dp", "tp"),
        P("dp", "tp"),
        P("dp", "tp"),
        P("dp", None),
        P("tp", "dp"),
        P(None, "tp"),
        P("tp"),
        P(),
        P(),
        P("tp"),
        P("tp"),
        P("tp"),
        P("tp"),
    )
    return jax.shard_map(
        per_device, mesh=mesh, in_specs=in_specs, out_specs=out_specs, check_vma=False
    )
```

profile of v0, /device:TPU:0, one launch (start us, length us, event | category | flops | bytes accessed | tf_op | source)
XLA Modules:
  0.0 191.0 jit_solution(10258307357448883939)
XLA Ops:
  0.7 0.8 copy.32
  1.4 0.8 copy.33
  2.2 0.7 slice_bitcast_fusion.1.edge
  2.9 0.7 broadcast_in_dim.23
  3.6 0.1 pad_add_fusion.ctx.where
  3.7 0.9 concatenate.12.shard
  4.6 25.9 %shard_map.279 = (bf16[4,4,48,1536]{3,2,1,0:T(8,128)(2,1)S(1)}, bf16[16,768]{1,0:T(8,128)(2,1)S(1)}) custom-call(bf16[48,1536]{1,0:T(8,128)(2,1)S(1)} %concatenate.12.shard, bf16[16,768]{1,0:T(8,128)(2,1)S(1)} %slice_bitcast_fusion.1.edge), custom_call_target="tpu_custom_call" | custom-call | tf_op jit(solution)/shard_map/pallas_call | solution.py:157
  30.5 0.0 copy-start
  30.5 1.4 copy-done
  31.9 0.7 select_maximum_fusion.2.heads
  32.6 0.7 fusion.conv
  33.3 0.0 copy-start.23
  33.4 11.7 %shard_map.280 = (bf16[1024,768]{1,0:T(8,128)(2,1)}, bf16[1024,640]{1,0:T(8,128)(2,1)S(1)}, f32[1024,640]{1,0:T(8,128)}, bf16[1024,640]{1,0:T(8,128)(2,1)S(1)}, ...) custom-call(s32[2]{0:T(128)S(1)} %pad_add_fusion.ctx.where, ...), custom_call_target="tpu_custom_call" | custom-call | tf_op jit(solution)/shard_map/pallas_call | solution.py:873
  45.1 1.2 copy-done.10
  46.2 2.4 %collective-permute-start = (f32[384,128]{1,0:T(8,128)S(1)}, f32[384,128]{1,0:T(8,128)S(1)}, u32[]{:S(2)}, u32[]{:S(2)}) collective-permute-start(f32[384,128]{1,0:T(8,128)S(1)} %get-tuple-element.75), channel_id=1, source_target_pairs={{0,4},{1,5},{2,6},{3,7},{8,12},{9,13},{10,14},{11,15},{16,20},{17,... | collective-permute-start | bytes 589832 | tf_op jit(solution)/shard_map/ppermute | solution.py:966
  48.6 0.0 copy-done.23
  48.7 5.1 %shard_map.281 = (f32[1024,384]{1,0:T(8,128)S(1)}, f32[1024,384]{1,0:T(8,128)S(1)}) custom-call(bf16[1024,640]{1,0:T(8,128)(2,1)S(1)} %get-tuple-element.66.vals, f32[1024,128]{1,0:T(8,128)S(1)} %get-tuple-element.67.cum, f32[4,8,256]{2,1,0:T(8,128)S(1)} %get-tuple-element.70.cum_t, f32[4,8,256]{2,1,0:T(8,128)S(1)} %get-tuple-element.71.step_t, ...), custom_call_target="tpu_custom_call" | custom-call | tf_op jit(solution)/shard_map/pallas_call | solution.py:873
  53.8 0.0 copy-done.21
  53.8 0.0 copy-start.4
  53.8 1.2 copy-done.4
  55.0 1.2 copy-done.9
  56.2 0.0 collective-permute-done.entering
  56.2 4.1 %shard_map.282 = (f32[1024,384]{1,0:T(8,128)S(1)}, f32[4,384,128]{2,1,0:T(8,128)S(1)}, f32[8,1024]{1,0:T(8,128)S(1)}) custom-call(bf16[1024,640]{1,0:T(8,128)(2,1)S(1)} %get-tuple-element.66.vals, f32[1024,384]{1,0:T(8,128)} %copy-done.9, f32[1024,384]{1,0:T(8,128)} %get-tuple-element.73.gate, f32[4,384,128]{2,1,0:T(8,128)S(1)} %get-tuple-element.74.fresh, ...), custom_call_target="tpu_custom_call" | custom-call | tf_op jit(solution)/shard_map/pallas_call | solution.py:873
  60.3 0.0 copy-start.8
  60.3 1.2 copy-done.8
  61.5 4.1 %shard_map.283.sums = f32[8,1024]{1,0:T(8,128)S(1)} custom-call(f32[8,1024]{1,0:T(8,128)S(1)} %get-tuple-element.79.part), custom_call_target="tpu_custom_call" | custom-call | tf_op jit(solution)/shard_map/pallas_call | solution.py:455
  65.6 0.0 copy-done.1
  65.6 5.4 %shard_map.284 = (bf16[1024,384]{1,0:T(8,128)(2,1)S(1)}, bf16[1024,384]{1,0:T(8,128)(2,1)S(1)}, bf16[1024,384]{1,0:T(8,128)(2,1)S(1)}, f32[4,384,128]{2,1,0:T(8,...) custom-call(f32[1024,384]{1,0:T(8,128)} %copy-done.8, f32[1024,384]{1,0:T(8,128)} %get-tuple-element.73.gate, ...), custom_call_target="tpu_custom_call" | custom-call | tf_op jit(solution)/shard_map/pallas_call | solution.py:873
  71.0 0.0 copy-start.13
  71.0 0.9 copy-done.13
  71.9 0.9 copy-done.15
  72.8 0.9 copy-done.17
  73.7 0.9 copy-done.19
  74.5 1.5 collective-permute-start.1
  76.0 0.8 slice.57.slopes
  76.8 1.1 copy-done.18
  77.9 1.1 copy-done.20
  79.0 12.2 %shard_map.285 = (f32[1024,384]{1,0:T(8,128)}, f32[1024,128]{1,0:T(8,128)S(1)}, f32[1024,128]{1,0:T(8,128)S(1)}, f32[1024,256]{1,0:T(8,128)S(1)}, bf16[1024,768]...) custom-call(bf16[1024,384]{1,0:T(8,128)(2,1)S(1)} %copy-done.20, bf16[1024,640]{1,0:T(8,128)(2,1)} %copy-done.1, ...), custom_call_target="tpu_custom_call" | custom-call | tf_op jit(solution)/shard_map/pallas_call | solution.py:873
  91.3 1.0 copy-done.12
  92.2 0.0 collective-permute-done.1.arriving
  92.2 0.0 copy-done.16
  92.2 0.0 copy-done.22
  92.2 0.0 copy-start.11
  92.3 0.0 copy-start.14
  92.3 6.4 %shard_map.286 = (f32[1024,384]{1,0:T(8,128)}, bf16[1024,256]{1,0:T(8,128)(2,1)S(1)}, bf16[1024,128]{1,0:T(8,128)(2,1)S(1)}, f32[8,128]{1,0:T(8,128)S(1)}) custom-call(bf16[1024,640]{1,0:T(8,128)(2,1)} %copy-done.1, f32[1024,128]{1,0:T(8,128)S(1)} %get-tuple-element.67.cum, f32[1024,128]{1,0:T(8,128)S(1)} %get-tuple-element.68.step_val, ...), custom_call_target="tpu_custom_call" | custom-call | tf_op jit(solution)/shard_map/pallas_call | solution.py:873
  98.7 0.7 slice.56.values
  99.4 19.6 %shard_map.287 = (bf16[1024,256]{1,0:T(8,128)(2,1)S(1)}, f32[16,384]{1,0:T(8,128)S(1)}, f32[16,640]{1,0:T(8,128)S(1)}, bf16[16,256]{1,0:T(8,128)(2,1)S(1)}) custom-call(bf16[1024,256]{1,0:T(8,128)(2,1)S(1)} %get-tuple-element.89.part, f32[16,384]{1,0:T(8,128)S(1)} %slice.56.values, f32[16,640]{1,0:T(8,128)S(1)} %slice.57.slopes), custom_call_target="tpu_custom_call" | custom-call | tf_op jit(solution)/shard_map/pallas_call | solution.py:490
  119.1 1.4 copy-done.6
  120.5 12.8 %shard_map.288 = (bf16[1024,768]{1,0:T(8,128)(2,1)S(1)}, bf16[768,1152]{1,0:T(8,128)(2,1)}, f32[24,384]{1,0:T(8,128)S(1)}) custom-call(s32[2]{0:T(128)S(1)} %pad_add_fusion.ctx.where, f32[1024,384]{1,0:T(8,128)S(1)} %copy-done.6, bf16[1024,256]{1,0:T(8,128)(2,1)S(1)} %get-tuple-element.91.state, f32[1024,640]{1,0:T(8,128)} %get-tuple-element.90.slope, ...), custom_call_target="tpu_custom_call" | custom-call | tf_op jit(solution)/shard_map/pallas_call | solution.py:873
  133.3 0.0 copy-done.7
  133.3 0.0 copy-start.5
  133.3 1.5 copy-done.5
  134.8 46.7 %shard_map.289 = (f32[48,1536]{1,0:T(8,128)S(1)}, f32[24,384]{1,0:T(8,128)S(1)}, bf16[1024,768]{1,0:T(8,128)(2,1)S(1)}, bf16[1024,768]{1,0:T(8,128)(2,1)S(1)}) custom-call(bf16[4,4,48,1152]{3,2,1,0:T(8,128)(2,1)S(1)} %bitcast.37, bf16[4,4,48,384]{3,2,1,0:T(8,128)(2,1)S(1)} %bitcast.39, f32[24,384]{1,0:T(8,128)S(1)} %get-tuple-element.105.small, ...), custom_call_target="tpu_custom_call" | custom-call | tf_op jit(solution)/shard_map/pallas_call | solution.py:396
  181.5 0.7 slice_bitcast_fusion
  182.2 0.6 slice.62
  182.8 0.6 slice.64
  183.4 0.6 slice_reduce_fusion
  184.0 0.6 slice.66
  184.6 0.5 slice_bitcast_fusion.2
  185.1 0.6 slice.67
  185.7 2.9 %shard_map.290 = f32[1024,768]{1,0:T(8,128)} custom-call(bf16[1024,768]{1,0:T(8,128)(2,1)S(1)} %get-tuple-element.109.normed, bf16[1024,768]{1,0:T(8,128)(2,1)S(1)} %bitcast.33, bf16[1024,768]{1,0:T(8,128)(2,1)S(1)} %bitcast.36, f32[8,768]{1,0:T(8,128)S(1)} %get-tuple-element.96.gain), custom_call_target="tpu_custom_call" | custom-call | tf_op jit(solution)/shard_map/pallas_call | solution.py:873
  188.6 0.7 copy.34
  189.3 0.6 dynamic_slice.3
  189.9 1.1 copy.36
  (25 shorter events, 0.1 us)
Async XLA Ops:
  30.5 1.4 copy-start
  33.3 15.3 %copy-start.23 = (f32[384]{0:T(512)S(1)}, f32[384]{0:T(512)}, u32[]{:S(2)}) copy-start(f32[384]{0:T(512)} %param.30) | copy-start | bytes 4612
  45.1 1.2 copy-start.10
  46.2 7.6 %copy-start.21 = (f32[1024,128]{1,0:T(8,128)}, f32[1024,128]{1,0:T(8,128)S(1)}, u32[]{:S(2)}) copy-start(f32[1024,128]{1,0:T(8,128)S(1)} %get-tuple-element.69.sig) | copy-start | bytes 1572868
  46.2 19.4 %copy-start.1 = (bf16[1024,640]{1,0:T(8,128)(2,1)}, bf16[1024,640]{1,0:T(8,128)(2,1)S(1)}, u32[]{:S(2)}) copy-start(bf16[1024,640]{1,0:T(8,128)(2,1)S(1)} %get-tuple-element.66.vals) | copy-start | bytes 3932164
  46.2 10.0 %collective-permute-start = (f32[384,128]{1,0:T(8,128)S(1)}, f32[384,128]{1,0:T(8,128)S(1)}, u32[]{:S(2)}, u32[]{:S(2)}) collective-permute-start(f32[384,128]{1,0:T(8,128)S(1)} %get-tuple-element.75), channel_id=1, source_target_pairs={{0,4},{1,5},{2,6},{3,7},{8,12},{9,13},{10,14},{11,15},{16,20},{17,... | collective-permute-start | bytes 589832 | tf_op jit(solution)/shard_map/ppermute | solution.py:966
  53.8 1.2 copy-start.4
  55.0 1.2 copy-start.9
  60.3 1.2 copy-start.8
  71.0 0.9 copy-start.13
  71.9 0.9 copy-start.15
  72.8 0.9 copy-start.17
  73.6 0.9 copy-start.19
  74.5 17.7 %collective-permute-start.1 = (f32[384,128]{1,0:T(8,128)S(1)}, f32[384,128]{1,0:T(8,128)S(1)}, u32[]{:S(2)}, u32[]{:S(2)}) collective-permute-start(f32[384,128]{1,0:T(8,128)S(1)} %get-tuple-element.81), channel_id=1, source_target_pairs={{4,0},{5,1},{6,2},{7,3},{12,8},{13,9},{14,10},{15,11},{20,16},{21,... | collective-permute-start | bytes 589832 | tf_op jit(solution)/shard_map/ppermute | solution.py:1021
  76.8 1.1 copy-start.18
  77.9 1.1 copy-start.20
  79.0 13.2 %copy-start.16 = (f32[4,384,128]{2,1,0:T(8,128)S(1)}, f32[4,384,128]{2,1,0:T(8,128)}, u32[]{:S(2)}) copy-start(f32[4,384,128]{2,1,0:T(8,128)} %copy-done.15) | copy-start | bytes 2359300
  79.0 13.2 %copy-start.22 = (f32[1024,128]{1,0:T(8,128)S(1)}, f32[1024,128]{1,0:T(8,128)}, u32[]{:S(2)}) copy-start(f32[1024,128]{1,0:T(8,128)} %copy-done.21) | copy-start | bytes 1572868
  91.3 1.0 copy-start.12
  92.2 26.8 %copy-start.11 = (bf16[1024,640]{1,0:T(8,128)(2,1)S(1)}, bf16[1024,640]{1,0:T(8,128)(2,1)}, u32[]{:S(2)}) copy-start(bf16[1024,640]{1,0:T(8,128)(2,1)} %copy-done.10) | copy-start | bytes 3932164
  92.3 26.8 %copy-start.14 = (bf16[1024,384]{1,0:T(8,128)(2,1)S(1)}, bf16[1024,384]{1,0:T(8,128)(2,1)}, u32[]{:S(2)}) copy-start(bf16[1024,384]{1,0:T(8,128)(2,1)} %copy-done.13) | copy-start | bytes 2359300
  119.1 1.4 copy-start.6
  120.5 12.8 %copy-start.2 = (bf16[1,1024,768]{2,1,0:T(8,128)(2,1)S(1)}, bf16[1,1024,768]{2,1,0:T(8,128)(2,1)}, u32[]{:S(2)}) copy-start(bf16[1,1024,768]{2,1,0:T(8,128)(2,1)} %param.16) | copy-start | bytes 4718596
  120.5 12.8 %copy-start.7 = (bf16[1024,768]{1,0:T(8,128)(2,1)S(1)}, bf16[1024,768]{1,0:T(8,128)(2,1)}, u32[]{:S(2)}) copy-start(bf16[1024,768]{1,0:T(8,128)(2,1)} %get-tuple-element.107.branch) | copy-start | bytes 4718596
  133.3 1.5 copy-start.5
  134.8 50.9 %copy-start.3 = (bf16[1,1024,768]{2,1,0:T(8,128)(2,1)S(1)}, bf16[1,1024,768]{2,1,0:T(8,128)(2,1)}, u32[]{:S(2)}) copy-start(bf16[1,1024,768]{2,1,0:T(8,128)(2,1)} %param.31) | copy-start | bytes 4718596
where the time goes:
time: 193 us; the launch traced here: 191 us
  Pallas kernels  157 us (81%)
  local copies, waits for them, and re-layouts  27.8 us (14%)
  starting transfers between devices  3.86 us (2%)
    pallas_call x8, Pallas kernels, on_blocks(): pl.pallas_call(kernel, grid=(BLOCKS,), in_specs=ins, out_specs=tuple((spe...  60.6 us
    pallas_call x1, Pallas kernels, final_sums(): pl.pallas_call(final_kernel, out_shape=(jax.ShapeDtypeStruct((ROWS, WIDE)...  46.7 us
    pallas_call x1, Pallas kernels, gather_weights(): pl.pallas_call(gather_kernel, out_shape=(jax.ShapeDtypeStruct((SIDE, SIDE...  25.9 us
    pallas_call x1, Pallas kernels, state_sum(): pl.pallas_call(state_sum_kernel, out_shape=(jax.ShapeDtypeStruct(part.sha...  19.6 us
    unnamed x51, local copies, waits for them, and re-layouts  18.4 us
    pallas_call x1, Pallas kernels, sum_all(): pl.pallas_call(sum_all_kernel, out_shape=jax.ShapeDtypeStruct(part.shape,...  4.14 us
  transfers between devices with their start and end apart: 2, of which 0 were waited for; matrix products, arithmetic and copies ran while one was open for 0% of the time, Pallas kernels for 9%

commit v1 on v0

v1 whole, which is shorter than its diff:
```python
import types

import jax
import jax.numpy as jnp
from jax import lax
from jax.experimental import pallas as pl
from jax.experimental.pallas import tpu as pltpu
from jax.sharding import PartitionSpec as P

D = 768
HEAD = 64
STATE = 128
CONV = 4
GROUP = 256
INNER = 1536


EPS = 1e-05
HIGH = lax.Precision.HIGHEST


MESH = pl.DeviceIdType.MESH
VM = pl.BlockSpec(memory_space=pltpu.VMEM)
SIDE = 4
ROWS = 48
WIDE = 1536
LOCAL = 384
DMA = pltpu.SemaphoreType.DMA
F32 = jnp.float32
BF16 = jnp.bfloat16


def params(ident, limit=20):
    return pltpu.CompilerParams(
        collective_id=ident, has_side_effects=True, vmem_limit_bytes=limit * 1024 * 1024
    )


def remote(source, target, send, recv, where):
    return pltpu.make_async_remote_copy(
        src_ref=source,
        dst_ref=target,
        send_sem=send,
        recv_sem=recv,
        device_id=where,
        device_id_type=MESH,
    )


def greet(peers):
    barrier = pltpu.get_barrier_semaphore()
    for where in peers:
        pl.semaphore_signal(barrier, inc=1, device_id=where, device_id_type=MESH)
    pl.semaphore_wait(barrier, len(peers))


def place():
    me = lax.axis_index("dp")
    z, y = lax.div(me, SIDE), lax.rem(me, SIDE)

    def along_y(hop):
        return {"dp": z * SIDE + lax.rem(y + hop, SIDE)}

    def along_z(hop):
        return {"dp": lax.rem(z + hop, SIDE) * SIDE + y}

    return z, y, along_y, along_z


def ahead(position, hop):
    return lax.rem(position + hop, SIDE)


class Gather:
    def __init__(self, shard, full, first, y_first, send, recv, slot):
        z, y, along_y, along_z = place()
        columns = pl.ds(first, LOCAL)
        self.send, self.recv, self.slot = send, recv, slot
        if y_first:
            self.position, self.along, near = z, along_z, along_y
            self.block = lambda at, sub: full.at[at, pl.ds(2 * sub, 2), :, columns]
        else:
            self.position, self.along, near = y, along_y, along_z
            self.block = lambda at, sub: full.at[pl.ds(2 * sub, 2), at, :, columns]
        self.near = [
            remote(
                shard.at[:, columns],
                full.at[z, y, :, columns],
                send.at[slot + hop],
                recv.at[slot + hop],
                near(hop + 1),
            )
            for hop in range(3)
        ]
        for item in self.near:
            item.start()

    def copy(self, position, sub, slot, hop):
        item = remote(
            self.block(position, sub),
            self.block(position, sub),
            self.send.at[self.slot + slot],
            self.recv.at[self.slot + slot],
            self.along(hop),
        )
        item.start()
        return item

    def turn(self):
        for item in self.near:
            item.wait_recv()
        self.direct = [
            self.copy(self.position, 0, 3, 1),
            self.copy(self.position, 1, 4, 3),
            self.copy(self.position, 1, 5, 1),
            self.copy(self.position, 0, 6, 3),
        ]

    def relay(self):
        self.direct[0].wait_recv()
        one = self.copy(ahead(self.position, 3), 0, 7, 1)
        self.direct[1].wait_recv()
        two = self.copy(ahead(self.position, 1), 1, 8, 3)
        self.relayed = [one, two]

    def finish(self):
        for item in self.direct[2:] + self.relayed:
            item.wait_recv()

    def close(self):
        for item in self.near + self.direct + self.relayed:
            item.wait_send()


class RingScatter:
    def __init__(self, block, load, held, passed, position, along, send, recv, first):
        self.block, self.load, self.held, self.passed = block, load, held, passed
        self.position, self.along = position, along
        self.send, self.recv, self.first = send, recv, first
        far, right, left = ahead(position, 2), ahead(position, 1), ahead(position, 3)
        self.direct = [
            self.copy(block(far, 0), 0, 1),
            self.copy(block(far, 1), 1, 3),
            self.copy(block(right, 1), 2, 1),
            self.copy(block(left, 0), 3, 3),
        ]
        for item in self.direct:
            item.start()

    def copy(self, source, slot, hop):
        return remote(
            source,
            self.held.at[slot],
            self.send.at[self.first + slot],
            self.recv.at[self.first + slot],
            self.along(hop),
        )

    def relay(self):
        right, left = ahead(self.position, 1), ahead(self.position, 3)
        self.direct[0].wait_recv()
        self.passed[0] = (self.held[0].astype(F32) + self.load(right, 0).astype(F32)).astype(BF16)
        one = self.copy(self.passed.at[0], 4, 1)
        one.start()
        self.direct[1].wait_recv()
        self.passed[1] = (self.held[1].astype(F32) + self.load(left, 1).astype(F32)).astype(BF16)
        two = self.copy(self.passed.at[1], 5, 3)
        two.start()
        self.relayed = [one, two]

    def total(self, sub):
        own = self.load(self.position, sub).astype(F32)
        if sub == 0:
            self.direct[3].wait_recv()
            self.relayed[0].wait_recv()
            return own + self.held[3].astype(F32) + self.held[4].astype(F32)
        self.direct[2].wait_recv()
        self.relayed[1].wait_recv()
        return own + self.held[2].astype(F32) + self.held[5].astype(F32)

    def finish(self):
        for item in self.direct + self.relayed:
            item.wait_send()


class PairSum:
    def __init__(self, part, out, half_in, over_out, over_in, send, recv, first):
        self.part, self.out = part, out
        self.half_in, self.over_out, self.over_in = half_in, over_out, over_in
        self.send, self.recv, self.first = send, recv, first
        me = lax.axis_index("tp")
        core, chip = lax.rem(me, 2), lax.div(me, 2)
        self.twin, self.across = {"tp": me + 1 - 2 * core}, {"tp": me + 2 - 4 * chip}
        size = part.shape[0] // 4

        def quarter(c, h):
            return pl.ds(pl.multiple_of((2 * c + h) * size, size), size)

        self.keep, self.give = quarter(core, chip), quarter(core, 1 - chip)
        self.sends = [
            self.copy(part.at[quarter(1 - core, 1 - chip)], half_in.at[0], 0, self.twin),
            self.copy(part.at[quarter(1 - core, chip)], half_in.at[1], 1, self.twin),
        ]

    def copy(self, source, target, slot, where):
        item = remote(
            source, target, self.send.at[self.first + slot], self.recv.at[self.first + slot], where
        )
        item.start()
        return item

    def cross(self):
        self.sends[0].wait_recv()
        self.over_out[...] = (
            self.part[self.give].astype(F32) + self.half_in[0].astype(F32)
        ).astype(BF16)
        self.sends.append(self.copy(self.over_out, self.over_in, 2, self.across))

    def close(self, base=None):
        self.sends[1].wait_recv()
        self.sends[2].wait_recv()
        total = self.part[self.keep].astype(F32) + self.half_in[1].astype(F32)
        total = total + self.over_in[...].astype(F32)
        if base is not None:
            total = total + base[self.keep].astype(F32)
        self.out[self.keep] = total.astype(BF16)
        mine = self.out.at[self.keep]
        self.sends.append(self.copy(mine, mine, 3, self.across))
        self.sends.append(self.copy(mine, mine, 4, self.twin))

    def relay(self):
        self.sends[3].wait_recv()
        other = self.out.at[self.give]
        self.sends.append(self.copy(other, other, 5, self.twin))

    def finish(self):
        self.sends[4].wait_recv()
        self.sends[5].wait_recv()
        for item in self.sends:
            item.wait_send()


def pair_scratch(rows, columns):
    return [
        pltpu.VMEM((2, rows // 4, columns), BF16),
        pltpu.VMEM((rows // 4, columns), BF16),
        pltpu.VMEM((rows // 4, columns), BF16),
    ]


def all_peers(along_y, along_z):
    me, partner = lax.axis_index("tp"), {"ctx": 1 - lax.axis_index("ctx")}
    hops = range(1, SIDE)
    tp_peers = [{"tp": ahead(me, hop)} for hop in hops]
    return [along_y(hop) for hop in hops], [along_z(hop) for hop in hops], partner, tp_peers


def spread(source, held, own, peers, send, recv, first):
    copies = [
        remote(source, held.at[own], send.at[first + hop], recv.at[first + hop], peer)
        for hop, peer in enumerate(peers)
    ]
    for item in copies:
        item.start()
    return copies


def fold(held, own, value, copies):
    held[own] = value
    for item in copies:
        item.wait_recv()
    return (held[0] + held[1]) + (held[2] + held[3])


class WeightSum:
    def __init__(self, grads, z_first, scratch, send, recv, first):
        self.held, self.passed, self.mid, self.second = scratch
        z, y, along_y, along_z = place()
        self.grads, self.send, self.recv, self.first = grads, send, recv, first
        if z_first:
            block = lambda at, sub: grads.at[at, pl.ds(2 * sub, 2)]
            load = lambda at, sub: grads[at, pl.ds(2 * sub, 2)]
            self.later, self.along = y, along_y
            self.ring = RingScatter(block, load, self.held, self.passed, z, along_z, send, recv, first)
        else:
            block = lambda at, sub: grads.at[pl.ds(2 * sub, 2), at]
            load = lambda at, sub: grads[pl.ds(2 * sub, 2), at]
            self.later, self.along = z, along_z
            self.ring = RingScatter(block, load, self.held, self.passed, y, along_y, send, recv, first)

    def turn(self):
        for sub in range(2):
            self.mid[2 * sub : 2 * sub + 2] = self.ring.total(sub).astype(BF16)
        self.copies = []
        for hop in range(1, SIDE):
            slot = self.first + 5 + hop
            item = remote(
                self.mid.at[ahead(self.later, hop)],
                self.second.at[self.later],
                self.send.at[slot],
                self.recv.at[slot],
                self.along(hop),
            )
            item.start()
            self.copies.append(item)

    def total(self):
        self.second[self.later] = self.mid[self.later]
        for item in self.copies:
            item.wait_recv()
        held = [self.second[index].astype(F32) for index in range(SIDE)]
        return (held[0] + held[1]) + (held[2] + held[3])

    def finish(self):
        self.ring.finish()
        for item in self.copies:
            item.wait_send()


def weight_scratch():
    return [
        pltpu.VMEM((6, 2, ROWS, LOCAL), BF16),
        pltpu.VMEM((2, 2, ROWS, LOCAL), BF16),
        pltpu.VMEM((SIDE, ROWS, LOCAL), BF16),
        pltpu.VMEM((SIDE, ROWS, LOCAL), BF16),
    ]


BLOCKS = 4
LIMIT = 20
MIX = LOCAL + 2 * STATE
THIN = MIX + 128
PROJ = THIN + LOCAL
PAIRS = 3


def dot(left, right, left_dim=1, right_dim=0, precision=None):
    return lax.dot_general(
        left,
        right,
        (((left_dim,), (right_dim,)), ((), ())),
        preferred_element_type=F32,
        precision=precision,
    )


def lanes(rows, columns=128):
    return lax.broadcasted_iota(jnp.int32, (rows, columns), 1)


def expand(per_head):
    first = lanes(per_head.shape[0]) < HEAD
    return jnp.concatenate(
        [
            jnp.where(first, per_head[:, 2 * j : 2 * j + 1], per_head[:, 2 * j + 1 : 2 * j + 2])
            for j in range(PAIRS)
        ],
        axis=1,
    )


def head_sums(wide):
    lane = lanes(wide.shape[0])
    total = jnp.zeros(lane.shape, F32)
    for j in range(PAIRS):
        pair = wide[:, 128 * j : 128 * j + 128]
        even = jnp.sum(jnp.where(lane < HEAD, pair, 0.0), axis=1, keepdims=True)
        odd = jnp.sum(jnp.where(lane < HEAD, 0.0, pair), axis=1, keepdims=True)
        total = jnp.where(lane == 2 * j, even, jnp.where(lane == 2 * j + 1, odd, total))
    return total


def by_head(row, states):
    return jnp.concatenate(
        [row[:, h : h + 1] * states[HEAD * h : HEAD * h + HEAD] for h in range(2 * PAIRS)], axis=0
    )


def lower():
    shape = (GROUP, GROUP)
    return lax.broadcasted_iota(jnp.int32, shape, 0) >= lax.broadcasted_iota(jnp.int32, shape, 1)


def decay_of(cum, cum_t, h, mask):
    return jnp.exp(jnp.where(mask, cum[:, h : h + 1] - cum_t[h : h + 1], -1e30))


def project_kernel(step, ctx, stream, edge, full, conv, heads, normed_o, pre_o, slope_o, vals_o,
                   step_o, sig_o, cum_o, cum_t_o, step_t_o, fresh_o, state_o, gain_o, padded):

    def normalise(rows):
        scale = lax.rsqrt(jnp.mean(rows * rows, axis=-1, keepdims=True) + EPS)
        return (rows * scale * gain_o[0:1]).astype(BF16)

    @pl.when(step == 0)
    def _():
        gain_o[...] = jnp.broadcast_to(full[:, MIX:THIN].astype(F32).T[6:7], gain_o.shape)
        rows = dot(normalise(edge[...].astype(F32)), full[:, :MIX])
        rows = rows * jnp.where(ctx[0] == 1, 1.0, 0.0)
        padded[0:8] = rows[8:16].astype(BF16).astype(F32)
        state_o[...] = jnp.zeros_like(state_o)

    @pl.when(step > 0)
    def _():
        padded[0:8] = padded[GROUP : GROUP + 8]

    normed = normalise(stream[...].astype(F32))
    normed_o[...] = normed
    projected = dot(normed, full[:, :THIN])
    pre = projected[:, :MIX].astype(BF16)
    pre_o[...] = pre
    padded[8:] = pre.astype(F32)
    conv_sum = conv[4:5] + sum(conv[k : k + 1] * padded[5 + k : 5 + k + GROUP] for k in range(CONV))
    sig = jax.nn.sigmoid(conv_sum)
    slope_o[...] = sig * (1.0 + conv_sum * (1.0 - sig))
    vals = (conv_sum * sig).astype(BF16)
    vals_o[...] = vals
    live = lanes(GROUP) < 2 * PAIRS
    raw = jnp.where(live, projected[:, MIX:THIN] + heads[0:1], 0.0)
    sig_o[...] = jnp.where(live, jax.nn.sigmoid(raw), 0.0)
    step_val = jnp.maximum(raw, 0.0) + jnp.log1p(jnp.exp(-jnp.abs(raw)))
    step_val = jnp.where(live, step_val, 0.0)
    step_o[...] = step_val
    log_rate = -jnp.exp(heads[1:2]) * step_val
    cum = dot(lower().astype(F32), log_rate, precision=HIGH)
    cum_o[...] = cum
    cum_t_o[0] = cum.T[0:8]
    step_t_o[0] = step_val.T[0:8]
    last = cum[GROUP - 1 :]
    scales = step_val * jnp.exp(last - cum)
    weighted = (vals[:, :LOCAL].astype(F32) * expand(scales)).astype(BF16)
    fresh = dot(weighted, vals[:, LOCAL : LOCAL + STATE], 0, 0)
    fresh_o[0] = fresh
    state_o[...] = by_head(jnp.exp(last), state_o[...]) + fresh


def inside_kernel(step, vals, cum, cum_t, step_t, heads, up, normed, full, local_o, back_o, gate_o):
    gate_o[...] = dot(normed[...], full[:, THIN:PROJ])
    back_o[...] = dot(up[...], full[:, PROJ:])
    keys, reads = vals[:, LOCAL : LOCAL + STATE], vals[:, LOCAL + STATE :]
    inner = dot(reads, keys, 1, 1)
    mask, first = lower(), lanes(GROUP) < HEAD
    skip = expand(heads[2:3])
    for j in range(PAIRS):
        here = slice(128 * j, 128 * j + 128)
        pair = vals[:, here]
        outs = []
        for h in (2 * j, 2 * j + 1):
            weights = inner * decay_of(cum, cum_t[0], h, mask) * step_t[0, h : h + 1]
            outs.append(dot(weights.astype(BF16), pair))
        local_o[:, here] = jnp.where(first, outs[0], outs[1]) + skip[:, here] * pair.astype(F32)


def sum_row(wide):
    folded = wide[:, :128] + wide[:, 128:256] + wide[:, 256:]
    return jnp.sum(folded.T, axis=0, keepdims=True)


def output_kernel(step, vals, local, gate, fresh, cum, entering, back, gain, ssd_o, states_o, sums_o,
                  state):
    @pl.when(step == 0)
    def _():
        state[...] = entering[...]

    here = state[...]
    states_o[0] = here
    state[...] = by_head(jnp.exp(cum[GROUP - 1 :]), here) + fresh[0]
    carried = dot(vals[:, LOCAL + STATE :], here.astype(BF16), 1, 1)
    ssd = local[...] + expand(jnp.exp(cum[...])) * carried
    ssd_o[...] = ssd
    gated = ssd * (gate[...] * jax.nn.sigmoid(gate[...]))
    sums_o[0:1] = sum_row(gated * gated)
    sums_o[1:2] = sum_row(back[...] * gain[...] * gated)
    sums_o[2:8] = jnp.zeros((6, GROUP), F32)


def gates_kernel(step, ssd, gate, back, sums, gain, vals, cum, full, normal_o, dy_o, dgate_o, read_o,
                 chain_o, dgain_o, branch_o):
    @pl.when(step == 0)
    def _():
        chain_o[...] = jnp.zeros_like(chain_o)
        dgain_o[...] = jnp.zeros_like(dgain_o)

    both = sums[...].T
    scale = lax.rsqrt(both[:, 0:1] / INNER + EPS)
    gate_val, ssd_val = gate[...], ssd[...]
    sig = jax.nn.sigmoid(gate_val)
    act = gate_val * sig
    gated = ssd_val * act
    normal = (gated * scale * gain[...]).astype(BF16)
    normal_o[...] = normal
    branch_o[...] = dot(normal, full[:, PROJ:], 1, 1).astype(BF16)
    grad_normal = back[...]
    dgain_o[0:1] += jnp.sum(grad_normal * gated * scale, axis=0, keepdims=True)
    dgated = scale * (grad_normal * gain[...]) - gated * (scale * scale * scale) * (
        both[:, 1:2] / INNER
    )
    dy = (dgated * act).astype(BF16)
    dy_o[...] = dy
    dgate_o[...] = (dgated * ssd_val * (sig * (1.0 + gate_val * (1.0 - sig)))).astype(BF16)
    carried = (dy.astype(F32) * expand(jnp.exp(cum[...]))).astype(BF16)
    read = dot(carried, vals[:, LOCAL + STATE :], 0, 0)
    read_o[0] = read
    chain_o[...] = by_head(jnp.exp(cum[GROUP - 1 :]), chain_o[...]) + read


def split_dot(wide, low, left_dim):
    high = wide.astype(BF16)
    rest = (wide - high.astype(F32)).astype(BF16)
    return dot(high, low, left_dim) + dot(rest, low, left_dim)


def blocks_kernel(step, dy, vals, cum, cum_t, step_val, step_t, states, heads, dval_o, dcum_o, dstep_o,
                  dstate_o, skip_o, skips, rows):

    @pl.when(step == 0)
    def _():
        skips[...] = jnp.zeros_like(skips)
        rows[...] = jnp.zeros_like(rows)

    dy_f, values_f = dy[...].astype(F32), vals[:, :LOCAL].astype(F32)
    skips[0:1] += jnp.sum(dy_f * values_f, axis=0, keepdims=True)
    keys, reads = vals[:, LOCAL : LOCAL + STATE], vals[:, LOCAL + STATE :]
    inner = dot(reads, keys, 1, 1)
    mask, lane = lower(), lanes(GROUP)
    first = lane < HEAD
    skip = expand(heads[2:3])
    dinner = jnp.zeros((GROUP, GROUP), F32)
    dcum = jnp.zeros((GROUP, 128), F32)
    for j in range(PAIRS):
        here = slice(128 * j, 128 * j + 128)
        pair, dy_pair = values_f[:, here], dy[:, here]
        outs = []
        for h in (2 * j, 2 * j + 1):
            own = jnp.where(first if h % 2 == 0 else ~first, pair, 0.0).astype(BF16)
            decays = decay_of(cum, cum_t[0], h, mask)
            scaled = dot(dy_pair, own, 1, 1) * decays
            step_row = step_t[0, h : h + 1]
            product = scaled * inner
            rows[h : h + 1] = jnp.sum(product, axis=0, keepdims=True)
            dcum = jnp.where(
                lane == h, jnp.sum(product * step_row, axis=1, keepdims=True), dcum
            )
            dinner = dinner + scaled * step_row
            outs.append(dot((inner * decays * step_row).astype(BF16), dy_pair, 0, 0))
        dval_o[:, here] = jnp.where(first, outs[0], outs[1]) + skip[:, here] * dy_f[:, here]
    dstep = rows[...].T
    dstep_o[...] = dstep
    low = states[0].astype(BF16)
    grad_exp = dy_f * expand(jnp.exp(cum[...]))
    dcum_o[...] = dcum - dstep * step_val[...] + head_sums(grad_exp * dot(reads, low, 1, 1))
    dstate_o[:, :STATE] = split_dot(dinner, reads, 0)
    dstate_o[:, STATE:] = dot(grad_exp.astype(BF16), low) + split_dot(dinner, keys, 1)

    @pl.when(step == BLOCKS - 1)
    def _():
        skip_o[...] = head_sums(skips[...])


def states_kernel(step, vals, cum, step_val, sig, states, read, arriving, heads, dval, dcum, dstep, dstate,
                  dval_o, state_o, low_o, heads_o, carry):
    @pl.when(step == 0)
    def _():
        carry[...] = arriving[...]
        heads_o[...] = jnp.zeros_like(heads_o)

    out = carry[...]
    last = cum[GROUP - 1 :]
    decay = jnp.exp(last)
    carry[...] = by_head(decay, out) + read[0]
    product = out * states[0]
    row = lanes(1)
    dlast = jnp.zeros((1, 128), F32)
    for h in range(2 * PAIRS):
        own = jnp.sum(product[HEAD * h : HEAD * h + HEAD], axis=0, keepdims=True)
        dlast = jnp.where(row == h, jnp.sum(own, axis=1, keepdims=True), dlast)
    dlast = dlast * decay
    fresh = out.astype(BF16)
    keys = vals[:, LOCAL : LOCAL + STATE]
    values_f = vals[:, :LOCAL].astype(F32)
    to_end = jnp.exp(last - cum[...])
    scales = step_val[...] * to_end
    wide = expand(scales)
    dweighted = dot(keys, fresh, 1, 1)
    dval_o[...] = dval[...] + dweighted * wide
    state_o[:, :STATE] = (
        dstate[:, :STATE] + dot((values_f * wide).astype(BF16), fresh)
    ).astype(BF16)
    state_o[:, STATE:] = dstate[:, STATE:].astype(BF16)
    dscales = head_sums(dweighted * values_f)
    spill = dscales * scales
    dlast = dlast + jnp.sum(spill, axis=0, keepdims=True)
    at_end = lax.broadcasted_iota(jnp.int32, (GROUP, 128), 0) == GROUP - 1
    full_cum = dcum[...] - spill + jnp.where(at_end, dlast, 0.0)
    drate = dot(lower().astype(F32), full_cum, 0, 0, precision=HIGH)
    rate = jnp.exp(heads[1:2])
    total_step = dstep[...] + dscales * to_end - rate * drate
    pre = total_step * sig[...]
    low_o[...] = pre.astype(BF16)
    heads_o[0:1] += jnp.sum(pre, axis=0, keepdims=True)
    heads_o[1:2] += -rate * jnp.sum(drate * step_val[...], axis=0, keepdims=True)


def weights_kernel(step, where, dval, state, slope, pre, dgate, dstep, normed, stream, full, gain, conv,
                   values_next, state_next, slope_next, dgain, heads, skip,
                   part_o, dvalue_o, dstate_o, small_o, padded, total):
    block = BLOCKS - 1 - step

    @pl.when(step == 0)
    def _():
        small_o[...] = jnp.zeros_like(small_o)
        ahead_of = jnp.concatenate([values_next[0:8], state_next[...].astype(F32)[0:8]], axis=1)
        padded[GROUP:] = ahead_of * slope_next[0:8] * jnp.where(where[0] == 0, 1.0, 0.0)
        padded[GROUP:] = jnp.where(
            lax.broadcasted_iota(jnp.int32, (8, MIX), 0) < CONV - 1, padded[GROUP:], 0.0
        )
        total[...] = jnp.zeros_like(total)

    @pl.when(step > 0)
    def _():
        padded[GROUP:] = padded[0:8]

    grad = jnp.concatenate([dval[...], state[...].astype(F32)], axis=1) * slope[...]
    padded[0:GROUP] = grad
    pre_f = pre[...].astype(F32)
    dinput = jnp.zeros((GROUP, MIX), F32)
    for k in range(CONV):
        moved = padded[CONV - 1 - k : CONV - 1 - k + GROUP]
        dinput = dinput + conv[k : k + 1] * moved
        taps = jnp.sum(moved * pre_f, axis=0, keepdims=True)
        small_o[k : k + 1] += taps[:, :LOCAL]
        small_o[6 + k : 7 + k, : 2 * STATE] += taps[:, LOCAL:]
    bias = jnp.sum(grad, axis=0, keepdims=True)
    small_o[4:5] += bias[:, :LOCAL]
    small_o[10:11, : 2 * STATE] += bias[:, LOCAL:]
    low = dinput.astype(BF16)
    rest = [dstep[...], dgate[...]]
    total[...] += dot(normed[...], jnp.concatenate([low, dstep[...]], axis=1), 0, 0)
    share = jnp.where(where[1] == block, 1.0, 0.0)
    once = (dinput[:, LOCAL:] * share).astype(BF16)
    part = dot(jnp.concatenate([low[:, :LOCAL], once] + rest, axis=1), full[:, :PROJ], 1, 1)
    part_o[...] = part.astype(BF16)
    source = stream[...].astype(F32)
    scale = lax.rsqrt(jnp.mean(source * source, axis=-1, keepdims=True) + EPS)
    dnorm = jnp.sum(part * source * scale, axis=0, keepdims=True)
    small_o[16:17] += dnorm[:, :LOCAL]
    small_o[17:18] += dnorm[:, LOCAL:]

    @pl.when(block == 0)
    def _():
        small_o[5:6] = dgain[0:1]
        small_o[11:12, :128] = heads[0:1]
        small_o[12:13, :128] = heads[1:2]
        small_o[13:14, :128] = skip[0:1]
        dvalue_o[...] = gridded(total[:, :LOCAL])
        dstate_o[...] = gridded(total[:, LOCAL:])


def last_kernel(normed, stream, up, gain, branch, value, state, gate, small,
                out, mixed, value_o, state_o, step_o, gate_o, taps_o, state_taps_o):
    step = pl.program_id(0)
    source, grad = stream[...].astype(F32), normed[...].astype(F32)
    scale = lax.rsqrt(jnp.mean(source * source, axis=-1, keepdims=True) + EPS)
    scaled = grad * gain[0:1]
    inner = jnp.sum(scaled * source, axis=1, keepdims=True) / D
    out[...] = up[...].astype(F32) + (
        scale * scaled - source * (scale * scale * scale) * inner
    )

    mixed[...] = branch[...]

    @pl.when(step == 0)
    def _():
        value_o[...] = value[...]
        gate_o[...] = gate[...]
        state_o[...] = state[:, : 2 * STATE]
        step_o[...] = state[:, 2 * STATE : 2 * STATE + step_o.shape[1]]
        taps_o[...] = small[0:4]
        state_taps_o[...] = small[6:10, : 2 * STATE]


def finish(normed, stream, up, gain, branch, value, state, gate, small, heads_here):
    by_block = pl.BlockSpec((GROUP, D), lambda g: (g, 0))

    def all_of(*shape):
        return pl.BlockSpec(shape, lambda g: (0, 0))

    owned = (ROWS, LOCAL)
    small_shapes = [
        owned, (ROWS, 2 * STATE), (ROWS, heads_here), owned, (CONV, LOCAL), (CONV, 2 * STATE)
    ]
    return pl.pallas_call(
        last_kernel,
        grid=(BLOCKS,),
        in_specs=[
            by_block,
            by_block,
            by_block,
            all_of(8, D),
            by_block,
            all_of(*owned),
            all_of(*owned),
            all_of(*owned),
            all_of(24, LOCAL),
        ],
        out_specs=(by_block, by_block, *[all_of(*shape) for shape in small_shapes]),
        out_shape=(
            jax.ShapeDtypeStruct(stream.shape, F32),
            jax.ShapeDtypeStruct(stream.shape, BF16),
            *[jax.ShapeDtypeStruct(shape, F32) for shape in small_shapes],
        ),
        compiler_params=pltpu.CompilerParams(vmem_limit_bytes=LIMIT * 1024 * 1024),
    )(normed, stream, up, gain, branch, value, state, gate, small)


def place_of(step, backward):
    return (BLOCKS - 1 - step) if backward else step


def tokens_spec(columns, backward=False):
    def view(ref, step):
        start = pl.multiple_of(place_of(step, backward) * GROUP, GROUP)
        return ref.at[pl.ds(start, GROUP)]

    return view


def cube_spec(rows, columns, backward=False):
    return lambda ref, step: ref.at[pl.ds(place_of(step, backward), 1)]


def row_spec(rows, backward=False):
    def view(ref, step):
        start = pl.multiple_of(place_of(step, backward) * GROUP, GROUP)
        return ref.at[:, pl.ds(start, GROUP)]

    return view


def whole(*shape):
    return lambda ref, step: ref


class Flat:
    def __init__(self, ref):
        self.ref = ref

    def __getitem__(self, key):
        found = self.ref[:, :, :, key[1]]
        return found.reshape(D, found.shape[-1])


def gridded(total):
    return total.astype(BF16).reshape(SIDE, SIDE, ROWS, total.shape[-1])


def sweep(kernel, pairs, start=0, stop=BLOCKS):
    def step(index, carry):
        kernel(index, *[item[1](item[0], index) if type(item) is tuple else item for item in pairs])
        return carry

    lax.fori_loop(start, stop, step, 0)


COUNT = BLOCKS * GROUP
HALF = COUNT // 2
KEPT = dict(
    full=((SIDE, SIDE, ROWS, WIDE), BF16),
    edge_in=((16, D), BF16),
    normed=((COUNT, D), BF16),
    pre=((COUNT, MIX), BF16),
    slope=((COUNT, MIX), F32),
    vals=((COUNT, MIX), BF16),
    step_val=((COUNT, 128), F32),
    sig=((COUNT, 128), F32),
    cum=((COUNT, 128), F32),
    cum_t=((BLOCKS, 8, GROUP), F32),
    step_t=((BLOCKS, 8, GROUP), F32),
    fresh=((BLOCKS, LOCAL, STATE), F32),
    leaving=((LOCAL, STATE), F32),
    padded=((GROUP + 8, MIX), F32),
    entering=((LOCAL, STATE), F32),
    local=((COUNT, LOCAL), F32),
    back=((COUNT, LOCAL), F32),
    gate=((COUNT, LOCAL), F32),
    ssd=((COUNT, LOCAL), F32),
    states=((BLOCKS, LOCAL, STATE), F32),
    sums=((8, COUNT), F32),
    sums_all=((8, COUNT), F32),
    sums_in=((4, 8, COUNT), F32),
    state=((LOCAL, STATE), F32),
    normal=((COUNT, LOCAL), BF16),
    dy=((COUNT, LOCAL), BF16),
    dgate=((COUNT, LOCAL), BF16),
    read=((BLOCKS, LOCAL, STATE), F32),
    returning=((LOCAL, STATE), F32),
    arriving=((LOCAL, STATE), F32),
    dgain=((8, LOCAL), F32),
    branch=((COUNT, D), BF16),
    dout_w=((SIDE, SIDE, ROWS, LOCAL), BF16),
    dgate_w=((SIDE, SIDE, ROWS, LOCAL), BF16),
    dcum=((COUNT, 128), F32),
    dstep=((COUNT, 128), F32),
    dstate=((COUNT, 2 * STATE), F32),
    skip=((8, 128), F32),
    skips=((8, LOCAL), F32),
    rows=((128, GROUP), F32),
    state_part=((COUNT, 2 * STATE), BF16),
    state_total=((COUNT, 2 * STATE), BF16),
    half_in=((HALF, 2 * STATE), BF16),
    chip_sum=((HALF, 2 * STATE), BF16),
    over_in=((HALF, 2 * STATE), BF16),
    values_in=((16, LOCAL), F32),
    slopes_in=((16, MIX), F32),
    state_in=((16, 2 * STATE), BF16),
    dstep_low=((COUNT, 128), BF16),
    head_rows=((8, 128), F32),
    part=((COUNT, D), BF16),
    dvalue_w=((SIDE, SIDE, ROWS, LOCAL), BF16),
    dstate_w=((SIDE, SIDE, ROWS, LOCAL), BF16),
    small=((24, LOCAL), F32),
    total=((D, 2 * LOCAL), F32),
    own=((4, ROWS, LOCAL), BF16),
    own_in=((4, ROWS, LOCAL), BF16),
    small_y=((SIDE, 24, LOCAL), F32),
    small_z=((SIDE, 24, LOCAL), F32),
    small_c=((24, LOCAL), F32),
    small_t=((SIDE, 8, LOCAL), F32),
    small_now=((3, 24, LOCAL), F32),
)
for name in ("gate", "out", "value", "state"):
    KEPT["held_" + name] = ((6, 2, ROWS, LOCAL), BF16)
    KEPT["passed_" + name] = ((2, 2, ROWS, LOCAL), BF16)
    KEPT["mid_" + name] = ((SIDE, ROWS, LOCAL), BF16)
    KEPT["second_" + name] = ((SIDE, ROWS, LOCAL), BF16)
for name in ("mixed", "normed"):
    KEPT["half_" + name] = ((2, COUNT // 4, D), BF16)
    KEPT["over_out_" + name] = ((COUNT // 4, D), BF16)
    KEPT["over_in_" + name] = ((COUNT // 4, D), BF16)
SLOTS = 116


def block_kernel(shard, edge, stream, up, conv, heads, gain, value_out, state_out, gate_out,
                 w_out_out, small_out, normed_out, mixed_out, gain_zero, *kept):
    by_name = dict(zip(KEPT, kept))
    m = types.SimpleNamespace(**by_name)
    send, recv, own_sem = kept[len(KEPT) :]
    z, y, along_y, along_z = place()
    ctx, tp = lax.axis_index("ctx"), lax.axis_index("tp")
    core, chip = lax.rem(tp, 2), lax.div(tp, 2)
    y_peers, z_peers, partner, tp_peers = all_peers(along_y, along_z)
    twin, across = {"tp": tp + 1 - 2 * core}, {"tp": tp + 2 - 4 * chip}
    beyond = {"ctx": 1 - ctx, "tp": tp + 1 - 2 * core}
    greet(y_peers + z_peers + [partner, beyond] + tp_peers)
    open_sends = []

    def to(source, target, slot, where):
        item = remote(source, target, send.at[slot], recv.at[slot], where)
        item.start()
        open_sends.append(item)
        return item

    full = Flat(m.full)
    at = tokens_spec(1)
    back_at = tokens_spec(1, True)
    cube, back_cube = cube_spec(1, 1), cube_spec(1, 1, True)
    row, back_row = row_spec(8), row_spec(8, True)

    def f(ref):
        return (ref, at)

    def r(ref):
        return (ref, back_at)

    def fc(ref):
        return (ref, cube)

    def rc(ref):
        return (ref, back_cube)

    gathers = [
        Gather(shard, m.full, LOCAL * index, index % 2 == 0, send, recv, 9 * index)
        for index in range(4)
    ]
    halo = to(edge, m.edge_in, 36, partner)
    keep = pltpu.make_async_copy(shard, m.full.at[z, y], own_sem)
    keep.start()
    keep.wait()
    gathers[0].turn()
    gathers[1].turn()
    gathers[0].relay()
    gathers[1].relay()
    gathers[2].turn()
    gathers[3].turn()
    gathers[0].finish()
    gathers[1].finish()
    halo.wait_recv()
    project = [
        [ctx], (stream, at), m.edge_in, full, conv, heads, f(m.normed), f(m.pre), f(m.slope),
        f(m.vals), f(m.step_val), f(m.sig), f(m.cum), fc(m.cum_t), fc(m.step_t), fc(m.fresh),
        m.leaving, gain_zero, m.padded,
    ]
    sweep(project_kernel, project, 0, 2)
    gathers[2].relay()
    gathers[3].relay()
    sweep(project_kernel, project, 2, 4)
    entering = to(m.leaving, m.entering, 37, partner)
    gathers[2].finish()
    gathers[3].finish()
    sweep(
        inside_kernel,
        [
            f(m.vals), f(m.cum), fc(m.cum_t), fc(m.step_t), heads, (up, at), f(m.normed), full,
            f(m.local), f(m.back), f(m.gate),
        ],
    )
    entering.wait_recv()
    m.state[...] = m.entering[...] * jnp.where(ctx == 1, 1.0, 0.0)
    sweep(
        output_kernel,
        [
            f(m.vals), f(m.local), f(m.gate), fc(m.fresh), f(m.cum), m.state, f(m.back), gain,
            f(m.ssd), fc(m.states), (m.sums, row), m.state,
        ],
    )
    to_tp = spread(m.sums, m.sums_in, tp, tp_peers, send, recv, 38)
    m.sums_all[...] = fold(m.sums_in, tp, m.sums[...], to_tp)
    open_sends.extend(to_tp)
    sweep(
        gates_kernel,
        [
            r(m.ssd), r(m.gate), r(m.back), (m.sums_all, back_row), gain, r(m.vals), r(m.cum),
            full, r(m.normal), r(m.dy), r(m.dgate), rc(m.read), m.returning, m.dgain,
            r(m.branch),
        ],
    )
    arriving = to(m.returning, m.arriving, 41, partner)
    mixed = PairSum(
        m.branch, mixed_out, m.half_mixed, m.over_out_mixed, m.over_in_mixed,
        send, recv, 42,
    )
    m.dout_w[...] = gridded(dot(up[...], m.normal[...], 0, 0))
    m.dgate_w[...] = gridded(dot(m.normed[...], m.dgate[...], 0, 0))
    mixed.cross()

    def weight_sum(name, z_first, slot):
        scratch = [by_name[kind + name] for kind in ("held_", "passed_", "mid_", "second_")]
        return WeightSum(by_name["d" + name + "_w"], z_first, scratch, send, recv, slot)

    gate_sum, out_sum = weight_sum("gate", True, 48), weight_sum("out", False, 57)
    blocks = [
        f(m.dy), f(m.vals), f(m.cum), fc(m.cum_t), f(m.step_val), fc(m.step_t), fc(m.states), heads,
        f(m.local), f(m.dcum), f(m.dstep), f(m.dstate), m.skip, m.skips, m.rows,
    ]
    sweep(blocks_kernel, blocks, 0, 2)
    gate_sum.ring.relay()
    out_sum.ring.relay()
    sweep(blocks_kernel, blocks, 2, 4)
    mixed.close(stream)
    gate_sum.turn()
    out_sum.turn()
    arriving.wait_recv()
    m.state[...] = m.arriving[...] * jnp.where(ctx == 0, 1.0, 0.0)
    sweep(
        states_kernel,
        [
            r(m.vals), r(m.cum), r(m.step_val), r(m.sig), rc(m.states), rc(m.read), m.state,
            heads, r(m.local), r(m.dcum), r(m.dstep), r(m.dstate), r(m.ssd), r(m.state_part),
            r(m.dstep_low), m.head_rows, m.state,
        ],
    )
    mine = pl.ds(pl.multiple_of(core * HALF, HALF), HALF)
    theirs = pl.ds(pl.multiple_of((1 - core) * HALF, HALF), HALF)
    to_twin = to(m.state_part.at[theirs], m.half_in, 66, twin)
    early = [
        to(m.ssd.at[0:16], m.values_in, 67, partner),
        to(m.slope.at[0:16], m.slopes_in, 68, partner),
    ]
    to_twin.wait_recv()
    m.chip_sum[...] = (
        m.state_part[mine].astype(F32) + m.half_in[...].astype(F32)
    ).astype(BF16)
    over = to(m.chip_sum, m.over_in, 69, across)
    m.own[0] = gate_sum.total().astype(BF16)
    m.own[1] = out_sum.total().astype(BF16)
    mixed.relay()
    over.wait_recv()
    total = m.state_total
    total[mine] = (m.chip_sum[...].astype(F32) + m.over_in[...].astype(F32)).astype(BF16)
    back = to(total.at[mine], total.at[mine], 70, twin)
    head = total.at[0:16]
    late = remote(head, m.state_in, send.at[71], recv.at[71], partner)
    late_twin = remote(head, m.state_in, send.at[72], recv.at[71], beyond)

    @pl.when(core == 0)
    def _():
        late.start()
        late_twin.start()

    pair = to(m.own.at[0:2], m.own_in.at[0:2], 73, partner)
    back.wait_recv()
    late.wait_recv()
    for item in early:
        item.wait_recv()
    sweep(
        weights_kernel,
        [
            [ctx, tp], r(m.ssd), r(m.state_total), r(m.slope), r(m.pre), r(m.dgate),
            r(m.dstep_low), r(m.normed), (stream, back_at), full, gain_zero, conv, m.values_in,
            m.state_in, m.slopes_in, m.dgain, m.head_rows, m.skip, r(m.part),
            m.dvalue_w, m.dstate_w, m.small, m.padded, m.total,
        ],
    )
    normed = PairSum(
        m.part, normed_out, m.half_normed, m.over_out_normed, m.over_in_normed,
        send, recv, 74,
    )
    value_sum, state_sum = weight_sum("value", True, 80), weight_sum("state", False, 89)
    small_now, small_z, small_y = m.small_now, m.small_z, m.small_y
    to_y = spread(m.small, small_y, y, y_peers, send, recv, 98)
    normed.cross()
    value_sum.ring.relay()
    state_sum.ring.relay()
    small_now[0] = fold(small_y, y, m.small[...], to_y)
    to_z = spread(small_now.at[0], small_z, z, z_peers, send, recv, 101)
    value_sum.turn()
    state_sum.turn()
    small_now[1] = fold(small_z, z, small_now[0], to_z)
    to_ctx = to(small_now.at[1], m.small_c, 104, partner)
    normed.close()
    m.own[2] = value_sum.total().astype(BF16)
    m.own[3] = state_sum.total().astype(BF16)
    pair_late = to(m.own.at[2:4], m.own_in.at[2:4], 105, partner)
    to_ctx.wait_recv()
    small_now[2] = small_now[1] + m.small_c[...]
    to_all = spread(small_now.at[2, pl.ds(16, 8)], m.small_t, tp, tp_peers, send, recv, 106)
    normed.relay()
    pair.wait_recv()
    gate_out[...] = m.own[0].astype(F32) + m.own_in[0].astype(F32)
    w_out_out[...] = m.own[1].astype(F32) + m.own_in[1].astype(F32)
    pair_late.wait_recv()
    value_out[...] = m.own[2].astype(F32) + m.own_in[2].astype(F32)
    state_out[...] = m.own[3].astype(F32) + m.own_in[3].astype(F32)
    small_out[0:16] = small_now[2, 0:16]
    small_out[16:24] = fold(m.small_t, tp, small_now[2, 16:24], to_all)
    normed.finish()
    mixed.finish()
    for item in gathers:
        item.close()
    for item in (gate_sum, out_sum, value_sum, state_sum):
        item.finish()

    @pl.when(core == 0)
    def _():
        late.wait_send()
        late_twin.wait_send()

    for item in open_sends + to_y + to_z + to_all:
        item.wait_send()


def per_device(
    stream,
    norm_gain,
    w_gate,
    w_value,
    w_step,
    w_state,
    w_out,
    conv_value,
    conv_value_bias,
    conv_state,
    conv_state_bias,
    step_bias,
    decay_log,
    skip_gain,
    inner_gain,
    cotangent,
):
    count = stream.shape[1]
    heads_here = step_bias.shape[0]
    rows, up = stream[0], cotangent[0]
    shard = jnp.concatenate(
        [
            w_value,
            w_state,
            w_step,
            norm_gain[:, None],
            jnp.zeros((ROWS, 128 - heads_here - 1), BF16),
            w_gate,
            w_out.T,
        ],
        axis=1,
    )
    edge = rows[count - 16 :]
    conv = jnp.concatenate(
        [
            jnp.concatenate([conv_value, conv_value_bias[None]], axis=0),
            jnp.concatenate([conv_state, conv_state_bias[None]], axis=0),
        ],
        axis=1,
    )
    conv = jnp.pad(conv, ((0, 3), (0, 0)))
    heads = jnp.pad(
        jnp.stack([step_bias, decay_log, skip_gain]), ((0, 5), (0, 128 - heads_here))
    )
    gain_one = inner_gain[None]
    owned = jax.ShapeDtypeStruct((ROWS, LOCAL), F32)
    wide = jax.ShapeDtypeStruct((COUNT, D), BF16)
    own_value, own_state, own_gate, own_out, totals, dnormed, mixed, gain_zero = pl.pallas_call(
        block_kernel,
        in_specs=[VM] * 7,
        out_specs=(VM,) * 8,
        out_shape=(
            owned,
            owned,
            owned,
            owned,
            jax.ShapeDtypeStruct((24, LOCAL), F32),
            wide,
            wide,
            jax.ShapeDtypeStruct((8, D), F32),
        ),
        scratch_shapes=[
            *[pltpu.VMEM(shape, dtype) for shape, dtype in KEPT.values()],
            DMA((SLOTS,)),
            DMA((SLOTS,)),
            DMA,
        ],
        compiler_params=params(1, 56),
    )(shard, edge, rows, up, conv, heads, gain_one)
    d_stream, mixed, value_w, state_w, step_w, gate_w, taps, state_taps = finish(
        dnormed, rows, up, gain_zero, mixed, own_value, own_state, own_gate, totals, heads_here
    )
    gain_total = totals[16:18].reshape(D)
    return (
        mixed[None],
        d_stream[None],
        lax.dynamic_slice_in_dim(gain_total, lax.axis_index("dp") * ROWS, ROWS),
        gate_w,
        value_w,
        step_w,
        state_w,
        own_out.T,
        taps,
        totals[4],
        state_taps,
        totals[10, : 2 * STATE],
        totals[11, :heads_here],
        totals[12, :heads_here],
        totals[13, :heads_here],
        totals[5],
    )


def solution(mesh):
    in_specs = (
        P("dp", "ctx", None),
        P("dp"),
        P("dp", "tp"),
        P("dp", "tp"),
        P("dp", "tp"),
        P("dp", None),
        P("tp", "dp"),
        P(None, "tp"),
        P("tp"),
        P(),
        P(),
        P("tp"),
        P("tp"),
        P("tp"),
        P("tp"),
        P("dp", "ctx", None),
    )
    out_specs = (
        P("dp", "ctx", None),
        P("dp", "ctx", None),
        P("dp"),
        P("dp", "tp"),
        P("dp", "tp"),
        P("dp", "tp"),
        P("dp", None),
        P("tp", "dp"),
        P(None, "tp"),
        P("tp"),
        P(),
        P(),
        P("tp"),
        P("tp"),
        P("tp"),
        P("tp"),
    )
    return jax.shard_map(
        per_device, mesh=mesh, in_specs=in_specs, out_specs=out_specs, check_vma=False
    )
```

time: 193 us -> 147 us (0.76)
  Pallas kernels: 157 us -> 122 us
  local copies, waits for them, and re-layouts: 27.8 us -> 19.9 us
  starting transfers between devices: 3.86 us -> 0 us
    pallas_call x12 -> x2, Pallas kernels: 157 us -> 122 us  [the longest x1 119 us: per_device(): pl.pallas_call(block_kernel, in_specs=[VM] * 7, out_specs=(VM,) * 8, out_...]
    unnamed x51 -> x23, local copies, waits for them, and re-layouts: 18.4 us -> 9.06 us
    ppermute x2 -> x0, starting transfers between devices: 3.86 us -> none  [the longest x1 2.4 us: per_device(): entering = lax.ppermute(leaving, 'ctx', [(0, 1)])]
    slice x7 -> x1, local copies, waits for them, and re-layouts: 4.08 us -> 1.35 us  [per_device(): edge = rows[count - 16:]]
  transfers between devices with their start and end apart: 2 -> 0, of which waited for: 0 -> 0; matrix products, arithmetic and copies ran while one was open for 0% -> 0% of each run, Pallas kernels for 9% -> 0%
where the time goes in v1:
time: 147 us; the launch traced here: 145 us
  Pallas kernels  122 us (83%)
  local copies, waits for them, and re-layouts  19.9 us (14%)
  other arithmetic  2.63 us (2%)
    pallas_call x1, Pallas kernels, per_device(): pl.pallas_call(block_kernel, in_specs=[VM] * 7, out_specs=(VM,) * 8, out_...  119 us
    unnamed x23, local copies, waits for them, and re-layouts  9.06 us
    pallas_call x1, Pallas kernels, finish(): pl.pallas_call(last_kernel, grid=(BLOCKS,), in_specs=[by_block, by_block,...  3.3 us

profile of v1, /device:TPU:0, one launch (start us, length us, event | category | flops | bytes accessed | tf_op | source)
XLA Modules:
  0.0 145.4 jit_solution(2186386816001514121)
XLA Ops:
  0.6 0.8 copy.32
  1.4 0.8 copy.33
  2.2 1.6 %concatenate.12.shard = bf16[48,1536]{1,0:T(8,128)(2,1)} concatenate(bf16[48,384]{1,0:T(8,128)(2,1)} %param.19, bf16[48,256]{1,0:T(8,128)(2,1)} %param.21, bf16[48,6]{1,0:T(8,128)(2,1)S(1)} %copy.32, bf16[48,1]{1,0:T(8,128)(2,1)S(1)} %copy.33, bf16[48,121]{1,0:T(8,128)(2,1)S(1)} %broadcast_in_dim.22, bf16[48,384]{1,0:T(8,128)(2,1)} %param.18, bf16[48,384]{1,0:T(8,128)(2,1)} %bitcast.25), dimensions={1} | concatenate | bytes 294912 | tf_op jit(solution)/shard_map/concatenate | solution.py:1083
  3.8 1.3 slice_bitcast_fusion.edge
  5.1 0.7 broadcast_in_dim.23
  5.8 1.3 fusion.conv
  7.1 1.3 select_maximum_fusion.2.heads
  8.4 1.2 broadcast_in_dim.25.gain
  9.7 0.0 copy-start
  9.7 0.0 copy-start.1
  9.7 118.9 %shard_map.279 = (f32[48,384]{1,0:T(8,128)}, f32[48,384]{1,0:T(8,128)}, f32[48,384]{1,0:T(8,128)}, f32[48,384]{1,0:T(8,128)}, f32[24,384]{1,0:T(8,128)}, /*index...) custom-call(bf16[48,1536]{1,0:T(8,128)(2,1)} %concatenate.12.shard, ...), custom_call_target="tpu_custom_call" | custom-call | tf_op jit(solution)/shard_map/pallas_call | solution.py:1110
  128.6 0.0 copy-done
  128.6 0.0 copy-done.1
  128.6 0.0 copy-start.2
  128.6 1.4 copy-done.2
  130.0 0.0 copy-start.3
  130.0 1.4 copy-done.3
  131.4 0.0 copy-start.4
  131.4 0.9 copy-done.4
  132.3 0.0 copy-start.5
  132.3 0.9 copy-done.5
  133.2 0.0 copy-start.6
  133.2 0.9 copy-done.6
  134.1 0.0 copy-start.7
  134.1 0.8 copy-done.7
  134.8 0.0 copy-start.8
  134.8 0.7 copy-done.8
  135.6 0.0 copy-start.9
  135.6 3.3 %shard_map.280 = (f32[1024,768]{1,0:T(8,128)}, bf16[1024,768]{1,0:T(8,128)(2,1)}, f32[48,384]{1,0:T(8,128)}, f32[48,256]{1,0:T(8,128)}, f32[48,6]{1,0:T(8,128)S(...) custom-call(bf16[1024,768]{1,0:T(8,128)(2,1)S(1)} %copy-done.2, bf16[1024,768]{1,0:T(8,128)(2,1)S(1)} %bitcast.21, ...), custom_call_target="tpu_custom_call" | custom-call | tf_op jit(solution)/shard_map/pallas_call | solution.py:692
  138.9 0.7 copy.34
  139.5 0.7 slice.29
  140.3 0.6 dynamic_slice.3
  140.8 1.3 slice_bitcast_fusion.1
  142.2 1.4 slice_reduce_fusion
  143.5 1.3 slice.31
  144.8 0.0 copy-done.9
  144.8 0.6 copy.36
  (2 shorter events, 0.0 us)
Async XLA Ops:
  9.7 118.9 %copy-start = (bf16[1,1024,768]{2,1,0:T(8,128)(2,1)S(1)}, bf16[1,1024,768]{2,1,0:T(8,128)(2,1)}, u32[]{:S(2)}) copy-start(bf16[1,1024,768]{2,1,0:T(8,128)(2,1)} %param.16) | copy-start | bytes 4718596
  9.7 118.9 %copy-start.1 = (bf16[1,1024,768]{2,1,0:T(8,128)(2,1)S(1)}, bf16[1,1024,768]{2,1,0:T(8,128)(2,1)}, u32[]{:S(2)}) copy-start(bf16[1,1024,768]{2,1,0:T(8,128)(2,1)} %param.31) | copy-start | bytes 4718596
  128.6 1.4 copy-start.2
  130.0 1.4 copy-start.3
  131.4 0.9 copy-start.4
  132.3 0.9 copy-start.5
  133.2 0.9 copy-start.6
  134.1 0.8 copy-start.7
  134.8 0.7 copy-start.8
  135.6 9.2 %copy-start.9 = (f32[48,384]{1,0:T(8,128)S(1)}, f32[48,384]{1,0:T(8,128)}, u32[]{:S(2)}) copy-start(f32[48,384]{1,0:T(8,128)} %get-tuple-element.45) | copy-start | bytes 221188

commit v2 on v1

--- a/solution.py
+++ b/solution.py
@@ -601,44 +601,70 @@
     heads_o[1:2] += -rate * jnp.sum(drate * step_val[...], axis=0, keepdims=True)
 
 
-def weights_kernel(step, where, dval, state, slope, pre, dgate, dstep, normed, stream, full, gain, conv,
-                   values_next, state_next, slope_next, dgain, heads, skip,
-                   part_o, dvalue_o, dstate_o, small_o, padded, total):
+def next_rows(block, extra):
+    keep = lax.broadcasted_iota(jnp.int32, block.shape, 0) < CONV - 1
+    return jnp.where(keep, block * extra, 0.0)
+
+
+def value_kernel(step, where, dval, slope, pre, dgate, dstep, normed, full, conv, values_next,
+                 slope_next, part_o, dvalue_o, small_o, padded, total):
+    @pl.when(step == 0)
+    def _():
+        small_o[...] = jnp.zeros_like(small_o)
+        own = values_next[0:8] * slope_next[0:8, :LOCAL]
+        padded[GROUP:, :LOCAL] = next_rows(own, jnp.where(where[0] == 0, 1.0, 0.0))
+        total[...] = jnp.zeros_like(total)
+
+    @pl.when(step > 0)
+    def _():
+        padded[GROUP:, :LOCAL] = padded[0:8, :LOCAL]
+
+    grad = dval[...] * slope[:, :LOCAL]
+    padded[0:GROUP, :LOCAL] = grad
+    pre_f = pre[:, :LOCAL].astype(F32)
+    dinput = jnp.zeros((GROUP, LOCAL), F32)
+    for k in range(CONV):
+        moved = padded[CONV - 1 - k : CONV - 1 - k + GROUP, :LOCAL]
+        dinput = dinput + conv[k : k + 1, :LOCAL] * moved
+        small_o[k : k + 1] += jnp.sum(moved * pre_f, axis=0, keepdims=True)
+    small_o[4:5] += jnp.sum(grad, axis=0, keepdims=True)
+    low = dinput.astype(BF16)
+    total[...] += dot(normed[...], jnp.concatenate([low, dstep[...]], axis=1), 0, 0)
+    part_o[...] = dot(low, full[:, :LOCAL], 1, 1) + dot(
+        jnp.concatenate([dstep[...], dgate[...]], axis=1), full[:, MIX:PROJ], 1, 1
+    )
+
+    @pl.when(step == BLOCKS - 1)
+    def _():
+        dvalue_o[...] = gridded(total[:, :LOCAL])
+
+
+def maps_kernel(step, where, state, slope, pre, normed, stream, full, conv, state_next, slope_next,
+                dgain, heads, skip, part_in, part_o, dstate_o, small_o, padded, total, thin):
     block = BLOCKS - 1 - step
 
     @pl.when(step == 0)
     def _():
-        small_o[...] = jnp.zeros_like(small_o)
-        ahead_of = jnp.concatenate([values_next[0:8], state_next[...].astype(F32)[0:8]], axis=1)
-        padded[GROUP:] = ahead_of * slope_next[0:8] * jnp.where(where[0] == 0, 1.0, 0.0)
-        padded[GROUP:] = jnp.where(
-            lax.broadcasted_iota(jnp.int32, (8, MIX), 0) < CONV - 1, padded[GROUP:], 0.0
-        )
+        own = state_next[...].astype(F32)[0:8] * slope_next[0:8, LOCAL:]
+        padded[GROUP:, LOCAL:] = next_rows(own, jnp.where(where[0] == 0, 1.0, 0.0))
         total[...] = jnp.zeros_like(total)
 
     @pl.when(step > 0)
     def _():
-        padded[GROUP:] = padded[0:8]
-
-    grad = jnp.concatenate([dval[...], state[...].astype(F32)], axis=1) * slope[...]
-    padded[0:GROUP] = grad
-    pre_f = pre[...].astype(F32)
-    dinput = jnp.zeros((GROUP, MIX), F32)
+        padded[GROUP:, LOCAL:] = padded[0:8, LOCAL:]
+
+    grad = state[...].astype(F32) * slope[:, LOCAL:]
+    padded[0:GROUP, LOCAL:] = grad
+    pre_f = pre[:, LOCAL:].astype(F32)
+    dinput = jnp.zeros((GROUP, 2 * STATE), F32)
     for k in range(CONV):
-        moved = padded[CONV - 1 - k : CONV - 1 - k + GROUP]
-        dinput = dinput + conv[k : k + 1] * moved
-        taps = jnp.sum(moved * pre_f, axis=0, keepdims=True)
-        small_o[k : k + 1] += taps[:, :LOCAL]
-        small_o[6 + k : 7 + k, : 2 * STATE] += taps[:, LOCAL:]
-    bias = jnp.sum(grad, axis=0, keepdims=True)
-    small_o[4:5] += bias[:, :LOCAL]
-    small_o[10:11, : 2 * STATE] += bias[:, LOCAL:]
-    low = dinput.astype(BF16)
-    rest = [dstep[...], dgate[...]]
-    total[...] += dot(normed[...], jnp.concatenate([low, dstep[...]], axis=1), 0, 0)
-    share = jnp.where(where[1] == block, 1.0, 0.0)
-    once = (dinput[:, LOCAL:] * share).astype(BF16)
-    part = dot(jnp.concatenate([low[:, :LOCAL], once] + rest, axis=1), full[:, :PROJ], 1, 1)
+        moved = padded[CONV - 1 - k : CONV - 1 - k + GROUP, LOCAL:]
+        dinput = dinput + conv[k : k + 1, LOCAL:] * moved
+        small_o[6 + k : 7 + k, : 2 * STATE] += jnp.sum(moved * pre_f, axis=0, keepdims=True)
+    small_o[10:11, : 2 * STATE] += jnp.sum(grad, axis=0, keepdims=True)
+    total[...] += dot(normed[...], dinput.astype(BF16), 0, 0)
+    once = (dinput * jnp.where(where[1] == block, 1.0, 0.0)).astype(BF16)
+    part = part_in[...] + dot(once, full[:, LOCAL:MIX], 1, 1)
     part_o[...] = part.astype(BF16)
     source = stream[...].astype(F32)
     scale = lax.rsqrt(jnp.mean(source * source, axis=-1, keepdims=True) + EPS)
@@ -652,8 +678,7 @@
         small_o[11:12, :128] = heads[0:1]
         small_o[12:13, :128] = heads[1:2]
         small_o[13:14, :128] = skip[0:1]
-        dvalue_o[...] = gridded(total[:, :LOCAL])
-        dstate_o[...] = gridded(total[:, LOCAL:])
+        dstate_o[...] = gridded(jnp.concatenate([total[...], thin[:, LOCAL:]], axis=1))
 
 
 def last_kernel(normed, stream, up, gain, branch, value, state, gate, small,
@@ -709,7 +734,7 @@
             jax.ShapeDtypeStruct(stream.shape, BF16),
             *[jax.ShapeDtypeStruct(shape, F32) for shape in small_shapes],
         ),
-        compiler_params=pltpu.CompilerParams(vmem_limit_bytes=LIMIT * 1024 * 1024),
+        compiler_params=pltpu.CompilerParams(vmem_limit_bytes=60 * 1024 * 1024),
     )(normed, stream, up, gain, branch, value, state, gate, small)
 
 
@@ -767,6 +792,9 @@
 KEPT = dict(
     full=((SIDE, SIDE, ROWS, WIDE), BF16),
     edge_in=((16, D), BF16),
+    conv=((8, MIX), F32),
+    heads=((8, 128), F32),
+    gain=((1, LOCAL), F32),
     normed=((COUNT, D), BF16),
     pre=((COUNT, MIX), BF16),
     slope=((COUNT, MIX), F32),
@@ -819,7 +847,9 @@
     dvalue_w=((SIDE, SIDE, ROWS, LOCAL), BF16),
     dstate_w=((SIDE, SIDE, ROWS, LOCAL), BF16),
     small=((24, LOCAL), F32),
-    total=((D, 2 * LOCAL), F32),
+    total=((D, LOCAL + 128), F32),
+    total_maps=((D, 2 * STATE), F32),
+    part_sum=((COUNT, D), F32),
     own=((4, ROWS, LOCAL), BF16),
     own_in=((4, ROWS, LOCAL), BF16),
     small_y=((SIDE, 24, LOCAL), F32),
@@ -840,7 +870,7 @@
 SLOTS = 116
 
 
-def block_kernel(shard, edge, stream, up, conv, heads, gain, value_out, state_out, gate_out,
+def block_kernel(shard, stream, up, taps_value, taps_state, singles, value_out, state_out, gate_out,
                  w_out_out, small_out, normed_out, mixed_out, gain_zero, *kept):
     by_name = dict(zip(KEPT, kept))
     m = types.SimpleNamespace(**by_name)
@@ -853,6 +883,14 @@
     beyond = {"ctx": 1 - ctx, "tp": tp + 1 - 2 * core}
     greet(y_peers + z_peers + [partner, beyond] + tp_peers)
     open_sends = []
+    conv, heads, gain = m.conv, m.heads, m.gain
+    conv[0:4, :LOCAL] = taps_value[...]
+    conv[0:4, LOCAL:] = taps_state[...]
+    conv[4:5] = singles[:, :MIX]
+    gain[...] = singles[:, MIX : MIX + LOCAL]
+    for index in range(3):
+        first = MIX + LOCAL + 128 * index
+        heads[index : index + 1] = singles[:, first : first + 128]
 
     def to(source, target, slot, where):
         item = remote(source, target, send.at[slot], recv.at[slot], where)
@@ -882,7 +920,7 @@
         Gather(shard, m.full, LOCAL * index, index % 2 == 0, send, recv, 9 * index)
         for index in range(4)
     ]
-    halo = to(edge, m.edge_in, 36, partner)
+    halo = to(stream.at[pl.ds(COUNT - 16, 16)], m.edge_in, 36, partner)
     keep = pltpu.make_async_copy(shard, m.full.at[z, y], own_sem)
     keep.start()
     keep.wait()
@@ -984,6 +1022,13 @@
     m.own[0] = gate_sum.total().astype(BF16)
     m.own[1] = out_sum.total().astype(BF16)
     mixed.relay()
+    for item in early:
+        item.wait_recv()
+    values = [
+        [ctx], r(m.ssd), r(m.slope), r(m.pre), r(m.dgate), r(m.dstep_low), r(m.normed), full, conv,
+        m.values_in, m.slopes_in, r(m.part_sum), m.dvalue_w, m.small, m.padded, m.total,
+    ]
+    sweep(value_kernel, values, 0, 3)
     over.wait_recv()
     total = m.state_total
     total[mine] = (m.chip_sum[...].astype(F32) + m.over_in[...].astype(F32)).astype(BF16)
@@ -998,24 +1043,23 @@
         late_twin.start()
 
     pair = to(m.own.at[0:2], m.own_in.at[0:2], 73, partner)
+    sweep(value_kernel, values, 3, 4)
+    value_sum = weight_sum("value", True, 80)
     back.wait_recv()
     late.wait_recv()
-    for item in early:
-        item.wait_recv()
     sweep(
-        weights_kernel,
+        maps_kernel,
         [
-            [ctx, tp], r(m.ssd), r(m.state_total), r(m.slope), r(m.pre), r(m.dgate),
-            r(m.dstep_low), r(m.normed), (stream, back_at), full, gain_zero, conv, m.values_in,
-            m.state_in, m.slopes_in, m.dgain, m.head_rows, m.skip, r(m.part),
-            m.dvalue_w, m.dstate_w, m.small, m.padded, m.total,
+            [ctx, tp], r(m.state_total), r(m.slope), r(m.pre), r(m.normed), (stream, back_at), full,
+            conv, m.state_in, m.slopes_in, m.dgain, m.head_rows, m.skip, r(m.part_sum), r(m.part),
+            m.dstate_w, m.small, m.padded, m.total_maps, m.total,
         ],
     )
     normed = PairSum(
         m.part, normed_out, m.half_normed, m.over_out_normed, m.over_in_normed,
         send, recv, 74,
     )
-    value_sum, state_sum = weight_sum("value", True, 80), weight_sum("state", False, 89)
+    state_sum = weight_sum("state", False, 89)
     small_now, small_z, small_y = m.small_now, m.small_z, m.small_y
     to_y = spread(m.small, small_y, y, y_peers, send, recv, 98)
     normed.cross()
@@ -1092,24 +1136,19 @@
         ],
         axis=1,
     )
-    edge = rows[count - 16 :]
-    conv = jnp.concatenate(
+    spare = jnp.zeros((128 - heads_here,), F32)
+    singles = jnp.concatenate(
         [
-            jnp.concatenate([conv_value, conv_value_bias[None]], axis=0),
-            jnp.concatenate([conv_state, conv_state_bias[None]], axis=0),
-        ],
-        axis=1,
-    )
-    conv = jnp.pad(conv, ((0, 3), (0, 0)))
-    heads = jnp.pad(
-        jnp.stack([step_bias, decay_log, skip_gain]), ((0, 5), (0, 128 - heads_here))
-    )
-    gain_one = inner_gain[None]
+            conv_value_bias, conv_state_bias, inner_gain, step_bias, spare, decay_log, spare,
+            skip_gain, spare,
+        ]
+    )[None]
+    taps_value, taps_state = conv_value, conv_state
     owned = jax.ShapeDtypeStruct((ROWS, LOCAL), F32)
     wide = jax.ShapeDtypeStruct((COUNT, D), BF16)
     own_value, own_state, own_gate, own_out, totals, dnormed, mixed, gain_zero = pl.pallas_call(
         block_kernel,
-        in_specs=[VM] * 7,
+        in_specs=[VM] * 6,
         out_specs=(VM,) * 8,
         out_shape=(
             owned,
@@ -1128,7 +1167,7 @@
             DMA,
         ],
         compiler_params=params(1, 56),
-    )(shard, edge, rows, up, conv, heads, gain_one)
+    )(shard, rows, up, taps_value, taps_state, singles)
     d_stream, mixed, value_w, state_w, step_w, gate_w, taps, state_taps = finish(
         dnormed, rows, up, gain_zero, mixed, own_value, own_state, own_gate, totals, heads_here
     )

time: 147 us -> 134 us (0.912)
  local copies, waits for them, and re-layouts: 19.9 us -> 11.8 us
  other arithmetic: 2.63 us -> 0 us
  Pallas kernels: 122 us -> 120 us
    unnamed x23 -> x5, local copies, waits for them, and re-layouts: 9.06 us -> 2.82 us
    pallas_call x1, Pallas kernels: 119 us -> 114 us  [per_device(): pl.pallas_call(block_kernel, in_specs=[VM] * 6, out_specs=(VM,) * 8, out_...]
    pallas_call x1, Pallas kernels: 3.3 us -> 6.19 us  [finish(): pl.pallas_call(last_kernel, grid=(BLOCKS,), in_specs=[by_block, by_block,...]
where the time goes in v2:
time: 134 us; the launch traced here: 133 us
  Pallas kernels  120 us (90%)
  local copies, waits for them, and re-layouts  11.8 us (9%)
    pallas_call x1, Pallas kernels, per_device(): pl.pallas_call(block_kernel, in_specs=[VM] * 6, out_specs=(VM,) * 8, out_...  114 us
    pallas_call x1, Pallas kernels, finish(): pl.pallas_call(last_kernel, grid=(BLOCKS,), in_specs=[by_block, by_block,...  6.19 us
    unnamed x5, local copies, waits for them, and re-layouts  2.82 us

profile of v2, /device:TPU:0, one launch (start us, length us, event | category | flops | bytes accessed | tf_op | source)
XLA Modules:
  0.0 132.7 jit_solution(3023300248710490305)
XLA Ops:
  0.6 0.8 copy.32
  1.4 0.8 copy.33
  2.2 1.6 %concatenate.6.shard = bf16[48,1536]{1,0:T(8,128)(2,1)} concatenate(bf16[48,384]{1,0:T(8,128)(2,1)} %param.19, bf16[48,256]{1,0:T(8,128)(2,1)} %param.21, bf16[48,6]{1,0:T(8,128)(2,1)S(1)} %copy.32, bf16[48,1]{1,0:T(8,128)(2,1)S(1)} %copy.33, bf16[48,121]{1,0:T(8,128)(2,1)S(1)} %broadcast_in_dim.19, bf16[48,384]{1,0:T(8,128)(2,1)} %param.18, bf16[48,384]{1,0:T(8,128)(2,1)} %bitcast.19), dimensions={1} | concatenate | bytes 294912 | tf_op jit(solution)/shard_map/concatenate | solution.py:1127
  3.8 0.8 concatenate.7
  4.6 0.6 broadcast_in_dim.21.singles
  5.2 114.0 %shard_map.279 = (f32[48,384]{1,0:T(8,128)}, f32[48,384]{1,0:T(8,128)}, f32[48,384]{1,0:T(8,128)}, f32[48,384]{1,0:T(8,128)}, f32[24,384]{1,0:T(8,128)}, /*index...) custom-call(bf16[48,1536]{1,0:T(8,128)(2,1)} %concatenate.6.shard, bf16[1024,768]{1,0:T(8,128)(2,1)} %bitcast.14, ...), custom_call_target="tpu_custom_call" | custom-call | tf_op jit(solution)/shard_map/pallas_call | solution.py:1149
  119.2 0.0 copy-start
  119.2 6.2 %shard_map.280 = (f32[1024,768]{1,0:T(8,128)}, bf16[1024,768]{1,0:T(8,128)(2,1)}, f32[48,384]{1,0:T(8,128)}, f32[48,256]{1,0:T(8,128)}, f32[48,6]{1,0:T(8,128)},...) custom-call(bf16[1024,768]{1,0:T(8,128)(2,1)} %get-tuple-element.32.normed, bf16[1024,768]{1,0:T(8,128)(2,1)} %bitcast.15, ...), custom_call_target="tpu_custom_call" | custom-call | tf_op jit(solution)/shard_map/pallas_call | solution.py:717
  125.4 1.4 %copy.34 = f32[48,6]{0,1:T(8,128)} copy(f32[48,6]{1,0:T(8,128)} %get-tuple-element.53) | data formatting | bytes 2304
  126.8 0.7 slice.21
  127.5 0.6 dynamic_slice.3
  128.1 1.3 slice_bitcast_fusion
  129.4 1.4 %slice_reduce_fusion = (f32[384]{0:T(512)}, f32[384]{0:T(512)}) fusion(f32[24,384]{1,0:T(8,128)} %get-tuple-element.38.small), kind=kLoop, calls=%fused_computation | loop fusion | bytes 6144 | tf_op jit(solution)/shard_map/slice | solution.py:1191
  130.8 1.3 slice.23
  132.0 0.0 copy-done
  132.0 0.6 copy.36
  (3 shorter events, 0.0 us)
Async XLA Ops:
  119.2 12.9 %copy-start = (f32[48,384]{1,0:T(8,128)S(1)}, f32[48,384]{1,0:T(8,128)}, u32[]{:S(2)}) copy-start(f32[48,384]{1,0:T(8,128)} %get-tuple-element.45) | copy-start | bytes 221188

commit v3 on v2

--- a/solution.py
+++ b/solution.py
@@ -681,8 +681,9 @@
         dstate_o[...] = gridded(jnp.concatenate([total[...], thin[:, LOCAL:]], axis=1))
 
 
-def last_kernel(normed, stream, up, gain, branch, value, state, gate, small,
-                out, mixed, value_o, state_o, step_o, gate_o, taps_o, state_taps_o):
+def last_kernel(normed, stream, up, gain, branch, value, state, gate, last, small,
+                out, mixed, value_o, state_o, step_o, gate_o, taps_o, state_taps_o, last_o, bias_o,
+                state_bias_o, inner_o, step_bias_o, decay_o, skip_o):
     step = pl.program_id(0)
     source, grad = stream[...].astype(F32), normed[...].astype(F32)
     scale = lax.rsqrt(jnp.mean(source * source, axis=-1, keepdims=True) + EPS)
@@ -702,17 +703,25 @@
         step_o[...] = state[:, 2 * STATE : 2 * STATE + step_o.shape[1]]
         taps_o[...] = small[0:4]
         state_taps_o[...] = small[6:10, : 2 * STATE]
-
-
-def finish(normed, stream, up, gain, branch, value, state, gate, small, heads_here):
+        last_o[...] = last[...]
+        bias_o[...] = small[4, :]
+        state_bias_o[...] = small[10, : 2 * STATE]
+        inner_o[...] = small[5, :]
+        step_bias_o[...] = small[11, : step_bias_o.shape[0]]
+        decay_o[...] = small[12, : decay_o.shape[0]]
+        skip_o[...] = small[13, : skip_o.shape[0]]
+
+
+def finish(normed, stream, up, gain, branch, value, state, gate, last, small, heads_here):
     by_block = pl.BlockSpec((GROUP, D), lambda g: (g, 0))
 
     def all_of(*shape):
-        return pl.BlockSpec(shape, lambda g: (0, 0))
+        return pl.BlockSpec(shape, lambda g: (0,) * len(shape))
 
     owned = (ROWS, LOCAL)
     small_shapes = [
-        owned, (ROWS, 2 * STATE), (ROWS, heads_here), owned, (CONV, LOCAL), (CONV, 2 * STATE)
+        owned, (ROWS, 2 * STATE), (ROWS, heads_here), owned, (CONV, LOCAL), (CONV, 2 * STATE),
+        owned, (LOCAL,), (2 * STATE,), (LOCAL,), (heads_here,), (heads_here,), (heads_here,),
     ]
     return pl.pallas_call(
         last_kernel,
@@ -726,6 +735,7 @@
             all_of(*owned),
             all_of(*owned),
             all_of(*owned),
+            all_of(*owned),
             all_of(24, LOCAL),
         ],
         out_specs=(by_block, by_block, *[all_of(*shape) for shape in small_shapes]),
@@ -735,7 +745,7 @@
             *[jax.ShapeDtypeStruct(shape, F32) for shape in small_shapes],
         ),
         compiler_params=pltpu.CompilerParams(vmem_limit_bytes=60 * 1024 * 1024),
-    )(normed, stream, up, gain, branch, value, state, gate, small)
+    )(normed, stream, up, gain, branch, value, state, gate, last, small)
 
 
 def place_of(step, backward):
@@ -1168,8 +1178,12 @@
         ],
         compiler_params=params(1, 56),
     )(shard, rows, up, taps_value, taps_state, singles)
-    d_stream, mixed, value_w, state_w, step_w, gate_w, taps, state_taps = finish(
-        dnormed, rows, up, gain_zero, mixed, own_value, own_state, own_gate, totals, heads_here
+    (
+        d_stream, mixed, value_w, state_w, step_w, gate_w, taps, state_taps, out_w, bias,
+        state_bias, inner_w, step_bias_w, decay_w, skip_w,
+    ) = finish(
+        dnormed, rows, up, gain_zero, mixed, own_value, own_state, own_gate, own_out, totals,
+        heads_here,
     )
     gain_total = totals[16:18].reshape(D)
     return (
@@ -1180,15 +1194,15 @@
         value_w,
         step_w,
         state_w,
-        own_out.T,
+        out_w.T,
         taps,
-        totals[4],
+        bias,
         state_taps,
-        totals[10, : 2 * STATE],
-        totals[11, :heads_here],
-        totals[12, :heads_here],
-        totals[13, :heads_here],
-        totals[5],
+        state_bias,
+        step_bias_w,
+        decay_w,
+        skip_w,
+        inner_w,
     )
 
 

time: 134 us -> 129 us (0.963)
  local copies, waits for them, and re-layouts: 11.8 us -> 7.23 us
    slice x2 -> x0, local copies, waits for them, and re-layouts: 2.64 us -> none  [the longest x1 1.38 us: per_device(): totals[5]]
    unnamed x5 -> x2, local copies, waits for them, and re-layouts: 2.82 us -> 2.19 us
where the time goes in v3:
time: 129 us; the launch traced here: 128 us
  Pallas kernels  120 us (93%)
  local copies, waits for them, and re-layouts  7.23 us (6%)
    pallas_call x1, Pallas kernels, per_device(): pl.pallas_call(block_kernel, in_specs=[VM] * 6, out_specs=(VM,) * 8, out_...  114 us
    pallas_call x1, Pallas kernels, finish(): pl.pallas_call(last_kernel, grid=(BLOCKS,), in_specs=[by_block, by_block,...  6.32 us

profile of v3, /device:TPU:0, one launch (start us, length us, event | category | flops | bytes accessed | tf_op | source)
XLA Modules:
  0.0 128.2 jit_solution(16861025161797128157)
XLA Ops:
  0.6 0.8 copy.32
  1.4 0.8 copy.33
  2.2 1.6 %concatenate.6.shard = bf16[48,1536]{1,0:T(8,128)(2,1)} concatenate(bf16[48,384]{1,0:T(8,128)(2,1)} %param.19, bf16[48,256]{1,0:T(8,128)(2,1)} %param.21, bf16[48,6]{1,0:T(8,128)(2,1)S(1)} %copy.32, bf16[48,1]{1,0:T(8,128)(2,1)S(1)} %copy.33, bf16[48,121]{1,0:T(8,128)(2,1)S(1)} %broadcast_in_dim.19, bf16[48,384]{1,0:T(8,128)(2,1)} %param.18, bf16[48,384]{1,0:T(8,128)(2,1)} %bitcast.11), dimensions={1} | concatenate | bytes 294912 | tf_op jit(solution)/shard_map/concatenate | solution.py:1137
  3.8 0.8 concatenate.7
  4.6 0.6 broadcast_in_dim.21.singles
  5.2 114.0 %shard_map.279 = (f32[48,384]{1,0:T(8,128)}, f32[48,384]{1,0:T(8,128)}, f32[48,384]{1,0:T(8,128)}, f32[48,384]{1,0:T(8,128)}, f32[24,384]{1,0:T(8,128)}, /*index...) custom-call(bf16[48,1536]{1,0:T(8,128)(2,1)} %concatenate.6.shard, bf16[1024,768]{1,0:T(8,128)(2,1)} %bitcast.7, ...), custom_call_target="tpu_custom_call" | custom-call | tf_op jit(solution)/shard_map/pallas_call | solution.py:1159
  119.2 6.3 %shard_map.280 = (f32[1024,768]{1,0:T(8,128)}, bf16[1024,768]{1,0:T(8,128)(2,1)}, f32[48,384]{1,0:T(8,128)}, f32[48,256]{1,0:T(8,128)}, f32[48,6]{1,0:T(8,128)},...) custom-call(bf16[1024,768]{1,0:T(8,128)(2,1)} %get-tuple-element.39., ...), custom_call_target="tpu_custom_call" | custom-call | tf_op jit(solution)/shard_map/pallas_call | solution.py:726
  125.5 1.4 %copy.34 = f32[48,6]{0,1:T(8,128)} copy(f32[48,6]{1,0:T(8,128)} %get-tuple-element.67) | data formatting | bytes 2304
  126.9 0.7 slice.3
  127.6 0.6 dynamic_slice.3
  (3 shorter events, 0.0 us)
